TPU v7x, 32 devices: a whole 2x2x4 slice. The times are simulated.
32 devices in a mesh: ctx: 4 (over y, core), grp: 8 (over z, x).
Axes of the slice: x: 2, y: 2, z: 4, core: 2. Of those that a mesh axis runs over, the one named last changes fastest.
Arguments:
- tokens: bfloat16 [4096, 4096], P(('ctx', 'grp')), may hold values from -6 to 6
- cotangent: bfloat16 [4096, 4096], P(('ctx', 'grp')), may hold values from -6 to 6
- conv_weight: float32 [3, 7, 4096], P(None, None, 'grp'), may hold values from -2 to 2
- residue: float32 [16, 4096], P(None, 'grp'), may hold values from -1.5 to 1.5
- decay_length: float32 [16, 4096], P(None, 'grp'), may hold values from 3 to 81920, as said below
- skip_gain: float32 [4096], P('grp'), may hold values from 0.5 to 1.5
Outputs:
- grad_tokens: bfloat16 [4096, 4096], P('ctx', 'grp')
Inputs may be any that keep to these rules, and one draw needn't show every extreme that they name: `decay_length`: each entry is a decay length in tokens.
All inputs are finite; a program needn't handle non-finite values.
Results may differ from a plain program's by a relative error of at most 0.001.
Values may be sent and summed in bfloat16 or wider, within the bound.
A program may use at most 128 MiB of HBM per device.

v0:
```python
import jax
import jax.numpy as jnp
from jax import lax
from jax.sharding import PartitionSpec as P


def shifted(block, axis, distance):
    devices = range(lax.axis_size(axis))
    route = [(i - distance, i) for i in devices if i - distance in devices]
    return lax.ppermute(block, axis, route)


def carry_ahead(shard_decay, local_sum):

    def relay_turn(turn_index, incoming):
        return shifted(shard_decay * incoming + local_sum, "ctx", 1)

    return lax.fori_loop(0, lax.axis_size("ctx") - 1, relay_turn, jnp.zeros_like(local_sum))


def carry_behind(shard_decay, local_sum):

    def relay_turn(turn_index, incoming):
        return shifted(shard_decay * incoming + local_sum, "ctx", -1)

    return lax.fori_loop(0, lax.axis_size("ctx") - 1, relay_turn, jnp.zeros_like(local_sum))


def power_table(inverse, exponents):
    return jnp.exp(-exponents[:, None, None] * inverse[None])


def depthwise(extended, weights, row_total):
    tap_count = weights.shape[0]
    return sum(
        (
            weights[offset]
            * extended[tap_count - 1 - offset : tap_count - 1 - offset + row_total].astype(
                jnp.float32
            )
            for offset in range(tap_count)
        )
    )


def within_block(blocks, lag_kernel, backward):
    width = blocks.shape[1]
    if backward:
        padded = jnp.pad(blocks, ((0, 0), (0, width - 1), (0, 0)))
        return sum(
            (
                lag_kernel[lag_step] * padded[:, lag_step : lag_step + width]
                for lag_step in range(width)
            )
        )
    padded = jnp.pad(blocks, ((0, 0), (width - 1, 0), (0, 0)))
    return sum(
        (
            lag_kernel[lag_step] * padded[:, width - 1 - lag_step : 2 * width - 1 - lag_step]
            for lag_step in range(width)
        )
    )


def pole_project(power_rows, blocks):
    return jnp.sum(power_rows[None] * blocks[:, :, None, :], axis=1)


def pole_mix(power_rows, states):
    return sum(
        (
            power_rows[:, pole_index][None] * states[:, pole_index][:, None]
            for pole_index in range(states.shape[1])
        )
    )


def per_device(tokens, cotangent, conv_weight, residue, decay_length, skip_gain):
    token_cols, grad_cols = (
        lax.all_to_all(tokens, "grp", split_axis=1, concat_axis=0, tiled=True),
        lax.all_to_all(cotangent, "grp", split_axis=1, concat_axis=0, tiled=True),
    )
    row_count, chan_count = token_cols.shape
    tap_count = conv_weight.shape[1]
    block_rows = min(128, row_count)
    block_count = row_count // block_rows
    inverse = 1.0 / decay_length
    modal_gain = residue * jnp.sqrt(-jnp.expm1(-2.0 * inverse))
    offsets = jnp.arange(block_rows, dtype=jnp.float32)
    lag_kernel = jnp.zeros((block_rows, chan_count), jnp.float32)
    for pole_index in range(residue.shape[0]):
        lag_kernel = lag_kernel + modal_gain[pole_index] * jnp.exp(
            -offsets[:, None] * inverse[pole_index]
        )
    enter_table = modal_gain * power_table(inverse, offsets + 1.0)
    end_table = power_table(inverse, block_rows - 1.0 - offsets)
    head_table = power_table(inverse, offsets)
    exit_table = modal_gain * power_table(inverse, block_rows - offsets)
    block_decay = jnp.exp(-block_rows * inverse)
    shard_decay = jnp.exp(-row_count * inverse)
    block_index = jnp.arange(block_count, dtype=jnp.float32)
    rows_ahead = shifted(token_cols[row_count - (tap_count - 1) :], "ctx", 1)
    extended = jnp.concatenate([rows_ahead, token_cols], 0)
    queries = depthwise(extended, conv_weight[0], row_count)
    source = (
        depthwise(extended, conv_weight[1], row_count)
        * depthwise(extended, conv_weight[2], row_count)
    ).reshape(block_count, block_rows, chan_count)
    block_ends = pole_project(end_table, source)

    def advance(carried, block_end):
        return (block_decay * carried + block_end, carried)

    local_last, local_starts = lax.scan(advance, jnp.zeros_like(inverse), block_ends)
    incoming = carry_ahead(shard_decay, local_last)
    starts = local_starts + jnp.exp(-(block_index * block_rows)[:, None, None] * inverse) * incoming
    long_out = (
        within_block(source, lag_kernel, False) + pole_mix(enter_table, starts) + skip_gain * source
    )
    long_out = long_out.reshape(row_count, chan_count)
    grad_out = grad_cols.astype(jnp.float32)
    upstream = (grad_out * queries).reshape(block_count, block_rows, chan_count)
    block_heads = pole_project(head_table, upstream)

    def retreat(carried, block_head):
        return (block_decay * carried + block_head, carried)

    local_first, local_nexts = lax.scan(retreat, jnp.zeros_like(inverse), block_heads, reverse=True)
    from_after = carry_behind(shard_decay, local_first)
    next_heads = (
        local_nexts
        + jnp.exp(-((block_count - 1.0 - block_index) * block_rows)[:, None, None] * inverse)
        * from_after
    )
    d_source = (
        within_block(upstream, lag_kernel, True)
        + pole_mix(exit_table, next_heads)
        + skip_gain * upstream
    )
    d_source = d_source.reshape(row_count, chan_count)
    d_queries = grad_out * long_out
    d_keys = d_source * depthwise(extended, conv_weight[2], row_count)
    d_values = d_source * depthwise(extended, conv_weight[1], row_count)
    streams = (d_queries, d_keys, d_values)
    rim_rows = jnp.stack([stream[: tap_count - 1] for stream in streams])
    behind = shifted(rim_rows, "ctx", -1)
    grad_rows = jnp.zeros((row_count, chan_count), jnp.float32)
    for stream_index in range(3):
        trailing = jnp.concatenate([streams[stream_index], behind[stream_index]], 0)
        grad_rows = grad_rows + sum(
            (
                conv_weight[stream_index, offset] * trailing[offset : offset + row_count]
                for offset in range(tap_count)
            )
        )
    return grad_rows.astype(jnp.bfloat16)


def solution(mesh):
    placed = (
        P(("ctx", "grp"), None),
        P(("ctx", "grp"), None),
        P(None, None, "grp"),
        P(None, "grp"),
        P(None, "grp"),
        P("grp"),
    )
    return jax.shard_map(
        per_device, mesh=mesh, in_specs=placed, out_specs=P("ctx", "grp"), check_vma=False
    )
```

profile of v0, /device:TPU:27, one launch (start us, length us, event | category | flops | bytes accessed | tf_op | source)
XLA Modules:
  0.0 273.5 jit_solution(10749103693539629523)
XLA Ops:
  0.0 2.3 copy.145
  2.3 5.6 %all-to-all-start.1 = ((bf16[128,8,512]{2,0,1:T(8,128)(2,1)}), bf16[128,8,512]{2,0,1:T(8,128)(2,1)S(1)}, u32[]{:S(2)}, u32[]{:S(2)}) async-start(bf16[128,8,512]{2,0,1:T(8,128)(2,1)} %bitcast.350), calls=%async_computation.1 | async-start | bytes 2097152 | tf_op jit(solution)/shard_map/all_to_all | solution.py:80
  15.3 1.1 copy.146
  16.4 4.5 %multiply_exponential_fusion.1 = (f32[128,16,512]{2,1,0:T(8,128)}, f32[128,16,512]{2,1,0:T(8,128)}, f32[128,16,512]{2,1,0:T(8,128)S(1)}, f32[128,16,512]{2,1,0:T(8,128)S(1)}) fusion(f32[128]{0:T(128)S(1)} %get-tuple-element.525, f32[16,512]{1,0:T(8,128)S(1)} %get-tuple-element.491, f32[128]{0:T(128)S(1)} %get-tuple-element.527, ...), kind=kLoop, calls=%fused_computation.279 | loop fusion | flops 6291456 | bytes 16844800 | tf_op jit(solution)/shard_map/exp | solution.py:30
  20.9 4.4 %fusion.593 = (f32[128,1,512]{2,1,0:T(1,128)}, f32[128,1,512]{2,1,0:T(1,128)}, f32[128,1,512]{2,1,0:T(1,128)}, f32[128,1,512]{2,1,0:T(1,128)}, f32[128,1,512]{2,...) fusion(f32[128,16,512]{2,1,0:T(8,128)S(1)} %get-tuple-element.487), kind=kLoop, calls=%fused_computation.1000 | loop fusion | bytes 8388608 | tf_op jit(solution)/shard_map/slice | solution.py:72
  25.3 4.6 %fusion.594 = (f32[128,1,512]{2,1,0:T(1,128)S(1)}, f32[128,1,512]{2,1,0:T(1,128)}, f32[128,1,512]{2,1,0:T(1,128)}, f32[128,1,512]{2,1,0:T(1,128)}, f32[128,1,512...) fusion(f32[128,16,512]{2,1,0:T(8,128)S(1)} %get-tuple-element.486), kind=kLoop, calls=%fused_computation.1001 | loop fusion | bytes 8388608 | tf_op jit(solution)/shard_map/slice | solution.py:72
  29.9 2.1 all-to-all-done.1
  32.0 5.4 %all-to-all-start = ((bf16[128,8,512]{2,0,1:T(8,128)(2,1)}), bf16[128,8,512]{2,0,1:T(8,128)(2,1)}, u32[]{:S(2)}, u32[]{:S(2)}) async-start(bf16[128,8,512]{2,0,1:T(8,128)(2,1)} %bitcast.351), calls=%async_computation | async-start | bytes 2097152 | tf_op jit(solution)/shard_map/all_to_all | solution.py:81
  38.0 4.8 %collective-permute-start.2 = (bf16[6,512]{1,0:T(8,128)(2,1)}, bf16[6,512]{1,0:T(8,128)(2,1)S(1)}, u32[]{:S(2)}, u32[]{:S(2)}) collective-permute-start(bf16[6,512]{1,0:T(8,128)(2,1)} %slice.2389), channel_id=1, source_target_pairs={{0,8},{8,16},{16,24},{1,9},{9,17},{17,25},{2,10},{10,18},{18,26},{... | collective-permute-start | bytes 18440 | tf_op jit(solution)/shard_map/ppermute | solution.py:10
  43.4 1.8 copy.163
  45.2 1.7 copy.164
  46.9 1.7 copy.165
  48.6 1.7 copy.166
  71.0 4.2 %fusion.590 = (f32[1024,512]{1,0:T(8,128)S(1)}, f32[1024,512]{1,0:T(8,128)}, f32[1024,512]{1,0:T(8,128)}) fusion(bf16[1024,512]{1,0:T(8,128)(2,1)S(1)} %bitcast.429, bf16[6,512]{1,0:T(8,128)(2,1)S(1)} %collective-permute-done.2, f32[512]{0:T(512)S(1)} %bitcast.507, f32[512]{0:T(512)S(1)} %bitcast.509, f32[512]{0:T(512)S(1)} %bitcast.511, ...), kind=kLoop, calls=%fused_computation.999 | loop fusion | flops 37748736 | bytes 7374848 | tf_op jit(solution)/shard_map/mul | solution.py:106
  75.2 3.1 %multiply_reduce_fusion.1 = f32[8,16,512]{2,1,0:T(8,128)} fusion(f32[8,128,512]{2,1,0:T(8,128)S(1)} %bitcast.424, f32[128,16,512]{2,1,0:T(8,128)S(1)} %copy-done.1), kind=kLoop, calls=%fused_computation.261 | loop fusion | flops 16711680 | bytes 6553600 | tf_op jit(solution)/shard_map/reduce_sum | solution.py:66
  78.3 6.5 %while.52 = (s32[]{:T(128)}, f32[16,512]{1,0:T(8,128)S(1)}, f32[8,16,512]{2,1,0:T(8,128)S(1)}, f32[16,512]{1,0:T(8,128)S(1)}, f32[8,16,512]{2,1,0:T(8,128)}, /*index=5*/s32[]{:T(128)}, s32[]{:T(128)}) while((s32[]{:T(128)}, f32[16,512]{1,0:T(8,128)S(1)}, f32[8,16,512]{2,1,0:T(8,128)S(1)}, f32[16,512]{1,0:T(8,128)S(1)}, ...), condition=%wide.region_2.3_spmd.clone, body=%wide.region_1.2_spmd.clone.sunk | while | flops 32771 | bytes 196704 | solution.py:114
  78.3 0.8 bitcast_add_fusion.4
  79.1 0.8 bitcast_add_fusion.4
  79.9 0.8 bitcast_add_fusion.4
  80.7 0.8 bitcast_add_fusion.4
  81.5 0.8 bitcast_add_fusion.4
  83.2 0.8 bitcast_add_fusion.4
  84.0 0.8 bitcast_add_fusion.4
  85.5 13.4 %while.50 = (s32[]{:T(128)}, f32[16,512]{1,0:T(8,128)S(1)}, f32[16,512]{1,0:T(8,128)S(1)}, f32[16,512]{1,0:T(8,128)S(1)}, s32[]{:T(128)}) while((s32[]{:T(128)}, f32[16,512]{1,0:T(8,128)S(1)}, f32[16,512]{1,0:T(8,128)S(1)}, f32[16,512]{1,0:T(8,128)S(1)}, s32[]{:T(128)}) %tuple.329), condition=%wide.region_4.5_spmd, body=%wide.region_3.4_spmd.sunk | while | flops 16386 | bytes 262245 | solution.py:18
  85.5 1.9 collective-permute-start
  87.4 1.2 collective-permute-done
  88.6 4.1 %collective-permute-start = (f32[16,512]{1,0:T(8,128)S(1)}, f32[16,512]{1,0:T(8,128)S(1)}, u32[]{:S(2)}, u32[]{:S(2)}) collective-permute-start(f32[16,512]{1,0:T(8,128)S(1)} %multiply_add_fusion.7), channel_id=1, source_target_pairs={{0,8},{8,16},{16,24},{1,9},{9,17},{17,25},{2,10},{10,18},{18,26},{... | collective-permute-start | bytes 98312 | tf_op jit(solution)/shard_map/while/body/eval_jaxpr/ppermute | solution.py:10
  92.7 1.0 collective-permute-done
  93.7 4.2 %collective-permute-start = (f32[16,512]{1,0:T(8,128)S(1)}, f32[16,512]{1,0:T(8,128)S(1)}, u32[]{:S(2)}, u32[]{:S(2)}) collective-permute-start(f32[16,512]{1,0:T(8,128)S(1)} %multiply_add_fusion.7), channel_id=1, source_target_pairs={{0,8},{8,16},{16,24},{1,9},{9,17},{17,25},{2,10},{10,18},{18,26},{... | collective-permute-start | bytes 98312 | tf_op jit(solution)/shard_map/while/body/eval_jaxpr/ppermute | solution.py:10
  97.9 1.0 collective-permute-done
  99.0 1.2 multiply_add_fusion.3
  100.7 48.8 %fusion.309 = f32[8,128,512]{2,1,0:T(8,128)} fusion(f32[8,128,512]{2,1,0:T(8,128)S(1)} %bitcast.425, f32[512]{0:T(512)} %param.19, f32[8,512]{1,0:T(8,128)S(1)} %bitcast.481, f32[128,512]{1,0:T(8,128)S(1)} %bitcast.447, f32[8,512]{1,0:T(8,128)S(1)} %bitcast.482, f32[128,512]{1,0:T(8,128)S(1)} %bitcast.448, f32[8,512]{1,0:T(8,128)S(1)} %bitcast.483, ...), kind=kLoop, calls=%fused_computation.616 | loop fusion | flops 151519232 | bytes 8914944 | tf_op jit(solution)/shard_map/add | solution.py:118
  149.7 4.7 %bitcast_multiply_fusion.2 = (f32[1024,512]{1,0:T(8,128)}, f32[1024,512]{1,0:T(8,128)S(1)}) fusion(bf16[128,8,512]{2,0,1:T(8,128)(2,1)} %all-to-all-done, f32[8,128,512]{2,1,0:T(8,128)} %fusion.309, bf16[1024,512]{1,0:T(8,128)(2,1)S(1)} %bitcast.430, bf16[6,512]{1,0:T(8,128)(2,1)S(1)} %collective-permute-done.2, f32[512]{0:T(512)S(1)} %bitcast.793, ...), kind=kLoop, calls=%fused_computation.906 | loop fusion | flops 21495808 | bytes 8409088 | tf_op jit(solution)/shard_map/mul | solution.py:141
  154.3 3.1 %multiply_reduce_fusion = f32[8,16,512]{2,1,0:T(8,128)} fusion(f32[8,128,512]{2,1,0:T(8,128)S(1)} %bitcast.426, f32[128,16,512]{2,1,0:T(8,128)S(1)} %copy-done), kind=kLoop, calls=%fused_computation.260 | loop fusion | flops 16711680 | bytes 6553600 | tf_op jit(solution)/shard_map/reduce_sum | solution.py:66
  158.2 11.3 %while.53 = (s32[]{:T(128)}, f32[16,512]{1,0:T(8,128)S(1)}, f32[8,16,512]{2,1,0:T(8,128)}, f32[16,512]{1,0:T(8,128)S(1)}, f32[8,16,512]{2,1,0:T(8,128)}, /*index=5*/s32[]{:T(128)}, s32[]{:T(128)}, s32[]{:T(128)}) while((s32[]{:T(128)}, f32[16,512]{1,0:T(8,128)S(1)}, f32[8,16,512]{2,1,0:T(8,128)}, f32[16,512]{1,0:T(8,128)S(1)}, ...), condition=%wide.region_7.8_spmd.clone, body=%wide.region_6.7_spmd.clone.sunk | while | flops 32772 | bytes 196724 | solution.py:128
  169.5 18.7 %while.51 = (s32[]{:T(128)}, f32[16,512]{1,0:T(8,128)S(1)}, f32[16,512]{1,0:T(8,128)S(1)}, f32[16,512]{1,0:T(8,128)S(1)}, s32[]{:T(128)}) while((s32[]{:T(128)}, f32[16,512]{1,0:T(8,128)S(1)}, f32[16,512]{1,0:T(8,128)S(1)}, f32[16,512]{1,0:T(8,128)S(1)}, s32[]{:T(128)}) %tuple.338), condition=%wide.region_9.10_spmd, body=%wide.region_8.9_spmd.sunk | while | flops 16386 | bytes 262245 | solution.py:26
  170.1 1.9 collective-permute-start.1
  172.0 4.1 %collective-permute-done.1 = f32[16,512]{1,0:T(8,128)S(1)} collective-permute-done((f32[16,512]{1,0:T(8,128)}, f32[16,512]{1,0:T(8,128)S(1)}, u32[]{:S(2)}, u32[]{:S(2)}) %collective-permute-start.1) | collective-permute-done | bytes 32800 | tf_op jit(solution)/shard_map/while/body/eval_jaxpr/ppermute | solution.py:10
  176.7 1.9 collective-permute-start.1
  178.6 3.5 %collective-permute-done.1 = f32[16,512]{1,0:T(8,128)S(1)} collective-permute-done((f32[16,512]{1,0:T(8,128)}, f32[16,512]{1,0:T(8,128)S(1)}, u32[]{:S(2)}, u32[]{:S(2)}) %collective-permute-start.1) | collective-permute-done | bytes 32800 | tf_op jit(solution)/shard_map/while/body/eval_jaxpr/ppermute | solution.py:10
  182.8 1.9 collective-permute-start.1
  184.7 3.5 %collective-permute-done.1 = f32[16,512]{1,0:T(8,128)S(1)} collective-permute-done((f32[16,512]{1,0:T(8,128)}, f32[16,512]{1,0:T(8,128)S(1)}, u32[]{:S(2)}, u32[]{:S(2)}) %collective-permute-start.1) | collective-permute-done | bytes 32800 | tf_op jit(solution)/shard_map/while/body/eval_jaxpr/ppermute | solution.py:10
  188.2 1.1 multiply_add_fusion.2
  189.8 65.8 %fusion.565 = f32[8,128,512]{2,1,0:T(8,128)S(1)} fusion(f32[8,128,512]{2,1,0:T(8,128)S(1)} %bitcast.427, f32[8,512]{1,0:T(8,128)S(1)} %bitcast.465, f32[128,512]{1,0:T(8,128)S(1)} %bitcast.431, f32[8,512]{1,0:T(8,128)S(1)} %bitcast.466, f32[128,512]{1,0:T(8,128)S(1)} %bitcast.432, f32[8,512]{1,0:T(8,128)S(1)} %bitcast.467, f32[128,512]{1,0:T(8,128)S(1)} %bitcast.433, ...), kind=kLoop, calls=%fused_computation.872 | loop fusion | flops 151519232 | bytes 8914944 | tf_op jit(solution)/shard_map/add | solution.py:136
  255.8 0.8 bitcast_multiply_fusion.1
  257.2 1.9 collective-permute-start.3
  259.1 3.5 %collective-permute-done.3 = f32[3,6,512]{2,1,0:T(8,128)S(1)} collective-permute-done((f32[3,6,512]{2,1,0:T(8,128)S(1)}, f32[3,6,512]{2,1,0:T(8,128)S(1)}, u32[]{:S(2)}, u32[]{:S(2)}) %collective-permute-start.3) | collective-permute-done | bytes 36896 | tf_op jit(solution)/shard_map/ppermute | solution.py:10
  262.8 10.7 %fusion.24 = bf16[1024,512]{1,0:T(8,128)(2,1)} fusion(f32[6,512]{1,0:T(8,128)S(1)} %get-tuple-element.461, f32[6,512]{1,0:T(8,128)S(1)} %get-tuple-element.462, f32[6,512]{1,0:T(8,128)S(1)} %get-tuple-element.460, f32[1024,512]{1,0:T(8,128)S(1)} %get-tuple-element.295, f32[1024,512]{1,0:T(8,128)S(1)} %get-tuple-element.294, f32[1024,512]{1,0:T(8,128)S(1)} %copy-done.2, ...), kind=kLoop, calls=%fused_computation.331 | loop fusion | flops 31457280 | bytes 7419904 | tf_op jit(solution)/shard_map/convert_element_type | solution.py:156
  (292 shorter events, 45.6 us)
Async XLA Ops:
  0.0 7.9 %copy-start.42 = (f32[16,512]{1,0:T(8,128)S(1)}, f32[16,512]{1,0:T(8,128)}, u32[]{:S(2)}) copy-start(f32[16,512]{1,0:T(8,128)} %param.18) | copy-start | bytes 98308
  0.0 7.9 %copy-start.43 = (f32[16,512]{1,0:T(8,128)S(1)}, f32[16,512]{1,0:T(8,128)}, u32[]{:S(2)}) copy-start(f32[16,512]{1,0:T(8,128)} %param.17) | copy-start | bytes 98308
  2.3 11.7 %copy-start.41 = (f32[3,7,512]{2,1,0:T(8,128)S(1)}, f32[3,7,512]{2,1,0:T(8,128)}, u32[]{:S(2)}) copy-start(f32[3,7,512]{2,1,0:T(8,128)} %param.16) | copy-start | bytes 129028
  2.3 13.0 %copy-start.37 = (bf16[128,4096]{1,0:T(8,128)(2,1)S(1)}, bf16[128,4096]{1,0:T(8,128)(2,1)}, u32[]{:S(2)}) copy-start(bf16[128,4096]{1,0:T(8,128)(2,1)} %param.15) | copy-start | bytes 3145732
  2.3 29.7 %all-to-all-start.1 = ((bf16[128,8,512]{2,0,1:T(8,128)(2,1)}), bf16[128,8,512]{2,0,1:T(8,128)(2,1)S(1)}, u32[]{:S(2)}, u32[]{:S(2)}) async-start(bf16[128,8,512]{2,0,1:T(8,128)(2,1)} %bitcast.350), calls=%async_computation.1 | async-start | bytes 2097152 | tf_op jit(solution)/shard_map/all_to_all | solution.py:80
  8.0 8.4 %copy-start.39 = (f32[16,512]{1,0:T(8,128)}, f32[16,512]{1,0:T(8,128)S(1)}, u32[]{:S(2)}) copy-start(f32[16,512]{1,0:T(8,128)S(1)} %get-tuple-element.491) | copy-start | bytes 98308
  32.0 117.6 %all-to-all-start = ((bf16[128,8,512]{2,0,1:T(8,128)(2,1)}), bf16[128,8,512]{2,0,1:T(8,128)(2,1)}, u32[]{:S(2)}, u32[]{:S(2)}) async-start(bf16[128,8,512]{2,0,1:T(8,128)(2,1)} %bitcast.351), calls=%async_computation | async-start | bytes 2097152 | tf_op jit(solution)/shard_map/all_to_all | solution.py:81
  38.0 32.8 %collective-permute-start.2 = (bf16[6,512]{1,0:T(8,128)(2,1)}, bf16[6,512]{1,0:T(8,128)(2,1)S(1)}, u32[]{:S(2)}, u32[]{:S(2)}) collective-permute-start(bf16[6,512]{1,0:T(8,128)(2,1)} %slice.2389), channel_id=1, source_target_pairs={{0,8},{8,16},{16,24},{1,9},{9,17},{17,25},{2,10},{10,18},{18,26},{... | collective-permute-start | bytes 18440 | tf_op jit(solution)/shard_map/ppermute | solution.py:10
  43.4 7.6 %copy-start.35 = (f32[128,1,512]{2,1,0:T(1,128)S(1)}, f32[128,1,512]{2,1,0:T(1,128)}, u32[]{:S(2)}) copy-start(f32[128,1,512]{2,1,0:T(1,128)} %get-tuple-element.268) | copy-start | bytes 786436
  43.4 8.4 %copy-start.34 = (f32[128,1,512]{2,1,0:T(1,128)S(1)}, f32[128,1,512]{2,1,0:T(1,128)}, u32[]{:S(2)}) copy-start(f32[128,1,512]{2,1,0:T(1,128)} %get-tuple-element.269) | copy-start | bytes 786436
  43.4 9.1 %copy-start.33 = (f32[128,1,512]{2,1,0:T(1,128)S(1)}, f32[128,1,512]{2,1,0:T(1,128)}, u32[]{:S(2)}) copy-start(f32[128,1,512]{2,1,0:T(1,128)} %get-tuple-element.270) | copy-start | bytes 786436
  43.4 9.9 %copy-start.32 = (f32[128,1,512]{2,1,0:T(1,128)S(1)}, f32[128,1,512]{2,1,0:T(1,128)}, u32[]{:S(2)}) copy-start(f32[128,1,512]{2,1,0:T(1,128)} %get-tuple-element.271) | copy-start | bytes 786436
  45.2 8.8 %copy-start.31 = (f32[128,1,512]{2,1,0:T(1,128)S(1)}, f32[128,1,512]{2,1,0:T(1,128)}, u32[]{:S(2)}) copy-start(f32[128,1,512]{2,1,0:T(1,128)} %get-tuple-element.272) | copy-start | bytes 786436
  46.9 7.8 %copy-start.30 = (f32[128,1,512]{2,1,0:T(1,128)S(1)}, f32[128,1,512]{2,1,0:T(1,128)}, u32[]{:S(2)}) copy-start(f32[128,1,512]{2,1,0:T(1,128)} %get-tuple-element.273) | copy-start | bytes 786436
  85.5 3.1 %collective-permute-start = (f32[16,512]{1,0:T(8,128)S(1)}, f32[16,512]{1,0:T(8,128)S(1)}, u32[]{:S(2)}, u32[]{:S(2)}) collective-permute-start(f32[16,512]{1,0:T(8,128)S(1)} %multiply_add_fusion.7), channel_id=1, source_target_pairs={{0,8},{8,16},{16,24},{1,9},{9,17},{17,25},{2,10},{10,18},{18,26},{... | collective-permute-start | bytes 98312 | tf_op jit(solution)/shard_map/while/body/eval_jaxpr/ppermute | solution.py:10
  88.6 5.1 %collective-permute-start = (f32[16,512]{1,0:T(8,128)S(1)}, f32[16,512]{1,0:T(8,128)S(1)}, u32[]{:S(2)}, u32[]{:S(2)}) collective-permute-start(f32[16,512]{1,0:T(8,128)S(1)} %multiply_add_fusion.7), channel_id=1, source_target_pairs={{0,8},{8,16},{16,24},{1,9},{9,17},{17,25},{2,10},{10,18},{18,26},{... | collective-permute-start | bytes 98312 | tf_op jit(solution)/shard_map/while/body/eval_jaxpr/ppermute | solution.py:10
  93.7 5.2 %collective-permute-start = (f32[16,512]{1,0:T(8,128)S(1)}, f32[16,512]{1,0:T(8,128)S(1)}, u32[]{:S(2)}, u32[]{:S(2)}) collective-permute-start(f32[16,512]{1,0:T(8,128)S(1)} %multiply_add_fusion.7), channel_id=1, source_target_pairs={{0,8},{8,16},{16,24},{1,9},{9,17},{17,25},{2,10},{10,18},{18,26},{... | collective-permute-start | bytes 98312 | tf_op jit(solution)/shard_map/while/body/eval_jaxpr/ppermute | solution.py:10
  100.7 48.9 %copy-start.44 = (f32[1,1,512]{2,1,0:T(1,128)S(1)}, f32[1,1,512]{2,1,0:T(1,128)}, u32[]{:S(2)}) copy-start(f32[1,1,512]{2,1,0:T(1,128)} %get-tuple-element.465) | copy-start | bytes 6148
  100.7 48.9 %copy-start.46 = (f32[1,1,512]{2,1,0:T(1,128)S(1)}, f32[1,1,512]{2,1,0:T(1,128)}, u32[]{:S(2)}) copy-start(f32[1,1,512]{2,1,0:T(1,128)} %get-tuple-element.466) | copy-start | bytes 6148
  100.7 48.9 %copy-start.48 = (f32[1,1,512]{2,1,0:T(1,128)S(1)}, f32[1,1,512]{2,1,0:T(1,128)}, u32[]{:S(2)}) copy-start(f32[1,1,512]{2,1,0:T(1,128)} %get-tuple-element.467) | copy-start | bytes 6148
  100.7 48.9 %copy-start.80 = (f32[1,1,512]{2,1,0:T(1,128)S(1)}, f32[1,1,512]{2,1,0:T(1,128)}, u32[]{:S(2)}) copy-start(f32[1,1,512]{2,1,0:T(1,128)} %get-tuple-element.482) | copy-start | bytes 6148
  100.7 48.9 %copy-start.82 = (f32[1,1,512]{2,1,0:T(1,128)S(1)}, f32[1,1,512]{2,1,0:T(1,128)}, u32[]{:S(2)}) copy-start(f32[1,1,512]{2,1,0:T(1,128)} %get-tuple-element.483) | copy-start | bytes 6148
  154.3 33.9 %copy-start.40 = (f32[16,512]{1,0:T(8,128)S(1)}, f32[16,512]{1,0:T(8,128)}, u32[]{:S(2)}) copy-start(f32[16,512]{1,0:T(8,128)} %copy-done.39) | copy-start | bytes 98308
  157.4 32.3 %copy-start.5 = (f32[128,1,512]{2,0,1:T(8,128)S(1)}, f32[128,1,512]{2,0,1:T(8,128)}, u32[]{:S(2)}) copy-start(f32[128,1,512]{2,0,1:T(8,128)} %copy.147) | copy-start | bytes 786436
  157.4 32.3 %copy-start.6 = (f32[128,1,512]{2,0,1:T(8,128)S(1)}, f32[128,1,512]{2,0,1:T(8,128)}, u32[]{:S(2)}) copy-start(f32[128,1,512]{2,0,1:T(8,128)} %copy.148) | copy-start | bytes 786436
  157.4 32.3 %copy-start.7 = (f32[128,1,512]{2,0,1:T(8,128)S(1)}, f32[128,1,512]{2,0,1:T(8,128)}, u32[]{:S(2)}) copy-start(f32[128,1,512]{2,0,1:T(8,128)} %copy.149) | copy-start | bytes 786436
  157.4 32.3 %copy-start.8 = (f32[128,1,512]{2,0,1:T(8,128)S(1)}, f32[128,1,512]{2,0,1:T(8,128)}, u32[]{:S(2)}) copy-start(f32[128,1,512]{2,0,1:T(8,128)} %copy.150) | copy-start | bytes 786436
  157.4 32.3 %copy-start.9 = (f32[128,1,512]{2,0,1:T(8,128)S(1)}, f32[128,1,512]{2,0,1:T(8,128)}, u32[]{:S(2)}) copy-start(f32[128,1,512]{2,0,1:T(8,128)} %copy.151) | copy-start | bytes 786436
  157.4 32.3 %copy-start.78 = (f32[1,512]{1,0:T(1,128)S(1)}, f32[1,512]{1,0:T(1,128)}, u32[]{:S(2)}) copy-start(f32[1,512]{1,0:T(1,128)} %get-tuple-element.390) | copy-start | bytes 6148
  157.4 32.3 %copy-start.79 = (f32[1,512]{1,0:T(1,128)S(1)}, f32[1,512]{1,0:T(1,128)}, u32[]{:S(2)}) copy-start(f32[1,512]{1,0:T(1,128)} %get-tuple-element.391) | copy-start | bytes 6148
  170.1 6.0 %collective-permute-start.1 = (f32[16,512]{1,0:T(8,128)}, f32[16,512]{1,0:T(8,128)S(1)}, u32[]{:S(2)}, u32[]{:S(2)}) collective-permute-start(f32[16,512]{1,0:T(8,128)} %multiply_add_fusion.8), channel_id=1, source_target_pairs={{8,0},{16,8},{24,16},{9,1},{17,9},{25,17},{10,2},{18,10},{26,18},{... | collective-permute-start | bytes 98312 | tf_op jit(solution)/shard_map/while/body/eval_jaxpr/ppermute | solution.py:10
  176.7 5.4 %collective-permute-start.1 = (f32[16,512]{1,0:T(8,128)}, f32[16,512]{1,0:T(8,128)S(1)}, u32[]{:S(2)}, u32[]{:S(2)}) collective-permute-start(f32[16,512]{1,0:T(8,128)} %multiply_add_fusion.8), channel_id=1, source_target_pairs={{8,0},{16,8},{24,16},{9,1},{17,9},{25,17},{10,2},{18,10},{26,18},{... | collective-permute-start | bytes 98312 | tf_op jit(solution)/shard_map/while/body/eval_jaxpr/ppermute | solution.py:10
  182.8 5.4 %collective-permute-start.1 = (f32[16,512]{1,0:T(8,128)}, f32[16,512]{1,0:T(8,128)S(1)}, u32[]{:S(2)}, u32[]{:S(2)}) collective-permute-start(f32[16,512]{1,0:T(8,128)} %multiply_add_fusion.8), channel_id=1, source_target_pairs={{8,0},{16,8},{24,16},{9,1},{17,9},{25,17},{10,2},{18,10},{26,18},{... | collective-permute-start | bytes 98312 | tf_op jit(solution)/shard_map/while/body/eval_jaxpr/ppermute | solution.py:10
  189.7 65.8 %copy-start.3 = (f32[1024,512]{1,0:T(8,128)S(1)}, f32[1024,512]{1,0:T(8,128)}, u32[]{:S(2)}) copy-start(f32[1024,512]{1,0:T(8,128)} %get-tuple-element.260) | copy-start | bytes 6291460
  189.7 65.8 %copy-start.4 = (f32[1024,512]{1,0:T(8,128)S(1)}, f32[1024,512]{1,0:T(8,128)}, u32[]{:S(2)}) copy-start(f32[1024,512]{1,0:T(8,128)} %get-tuple-element.261) | copy-start | bytes 6291460
  255.6 7.0 %copy-start.45 = (f32[1,1,512]{2,1,0:T(1,128)S(1)}, f32[1,1,512]{2,1,0:T(1,128)}, u32[]{:S(2)}) copy-start(f32[1,1,512]{2,1,0:T(1,128)} %get-tuple-element.465) | copy-start | bytes 6148
  255.6 7.0 %copy-start.47 = (f32[1,1,512]{2,1,0:T(1,128)S(1)}, f32[1,1,512]{2,1,0:T(1,128)}, u32[]{:S(2)}) copy-start(f32[1,1,512]{2,1,0:T(1,128)} %get-tuple-element.466) | copy-start | bytes 6148
  255.6 7.0 %copy-start.49 = (f32[1,1,512]{2,1,0:T(1,128)S(1)}, f32[1,1,512]{2,1,0:T(1,128)}, u32[]{:S(2)}) copy-start(f32[1,1,512]{2,1,0:T(1,128)} %get-tuple-element.467) | copy-start | bytes 6148
  255.6 7.0 %copy-start.51 = (f32[1,1,512]{2,1,0:T(1,128)S(1)}, f32[1,1,512]{2,1,0:T(1,128)}, u32[]{:S(2)}) copy-start(f32[1,1,512]{2,1,0:T(1,128)} %get-tuple-element.468) | copy-start | bytes 6148
  255.6 7.0 %copy-start.53 = (f32[1,1,512]{2,1,0:T(1,128)S(1)}, f32[1,1,512]{2,1,0:T(1,128)}, u32[]{:S(2)}) copy-start(f32[1,1,512]{2,1,0:T(1,128)} %get-tuple-element.469) | copy-start | bytes 6148
  255.7 7.0 %copy-start.55 = (f32[1,1,512]{2,1,0:T(1,128)S(1)}, f32[1,1,512]{2,1,0:T(1,128)}, u32[]{:S(2)}) copy-start(f32[1,1,512]{2,1,0:T(1,128)} %get-tuple-element.470) | copy-start | bytes 6148
  255.7 7.0 %copy-start.57 = (f32[1,1,512]{2,1,0:T(1,128)S(1)}, f32[1,1,512]{2,1,0:T(1,128)}, u32[]{:S(2)}) copy-start(f32[1,1,512]{2,1,0:T(1,128)} %get-tuple-element.471) | copy-start | bytes 6148
  255.7 7.0 %copy-start.59 = (f32[1,1,512]{2,1,0:T(1,128)S(1)}, f32[1,1,512]{2,1,0:T(1,128)}, u32[]{:S(2)}) copy-start(f32[1,1,512]{2,1,0:T(1,128)} %get-tuple-element.472) | copy-start | bytes 6148
  255.7 7.0 %copy-start.61 = (f32[1,1,512]{2,1,0:T(1,128)S(1)}, f32[1,1,512]{2,1,0:T(1,128)}, u32[]{:S(2)}) copy-start(f32[1,1,512]{2,1,0:T(1,128)} %get-tuple-element.473) | copy-start | bytes 6148
  255.7 7.0 %copy-start.63 = (f32[1,1,512]{2,1,0:T(1,128)S(1)}, f32[1,1,512]{2,1,0:T(1,128)}, u32[]{:S(2)}) copy-start(f32[1,1,512]{2,1,0:T(1,128)} %get-tuple-element.474) | copy-start | bytes 6148
  255.7 7.0 %copy-start.65 = (f32[1,1,512]{2,1,0:T(1,128)S(1)}, f32[1,1,512]{2,1,0:T(1,128)}, u32[]{:S(2)}) copy-start(f32[1,1,512]{2,1,0:T(1,128)} %get-tuple-element.475) | copy-start | bytes 6148
  255.7 7.0 %copy-start.67 = (f32[1,1,512]{2,1,0:T(1,128)S(1)}, f32[1,1,512]{2,1,0:T(1,128)}, u32[]{:S(2)}) copy-start(f32[1,1,512]{2,1,0:T(1,128)} %get-tuple-element.476) | copy-start | bytes 6148
  257.2 5.4 %collective-permute-start.3 = (f32[3,6,512]{2,1,0:T(8,128)S(1)}, f32[3,6,512]{2,1,0:T(8,128)S(1)}, u32[]{:S(2)}, u32[]{:S(2)}) collective-permute-start(f32[3,6,512]{2,1,0:T(8,128)S(1)} %pad_maximum_fusion.4), channel_id=1, source_target_pairs={{8,0},{16,8},{24,16},{9,1},{17,9},{25,17},{10,2},{18,10},{26,18},{... | collective-permute-start | bytes 110600 | tf_op jit(solution)/shard_map/ppermute | solution.py:10
  (46 other events, 235.5 us)
where the time goes:
time: 276 us; the launch traced here: 273 us
  other arithmetic  169 us (61%)
  local copies, waits for them, and re-layouts  49.1 us (18%)
  starting transfers between devices  33.7 us (12%)
  waiting for transfers between devices  19.9 us (7%)
    add x1, other arithmetic, per_device(): within_block(upstream, lag_kernel, True) + pole_mix(exit_table, next_heads)  65.8 us
    add x1, other arithmetic, per_device(): within_block(source, lag_kernel, False) + pole_mix(enter_table, starts)  48.8 us
    unnamed x232, local copies, waits for them, and re-layouts  28.9 us
    ppermute x8, starting transfers between devices, shifted(): return lax.ppermute(block, axis, route)  22.7 us
    ppermute x8, waiting for transfers between devices, shifted(): return lax.ppermute(block, axis, route)  17.8 us
    convert_element_type x1, other arithmetic, per_device(): return grad_rows.astype(jnp.bfloat16)  10.7 us
    slice x2, local copies, waits for them, and re-layouts, pole_mix(): power_rows[:, pole_index][None] * states[:, pole_index][:, None]  8.98 us
    add x8, other arithmetic, advance(): return (block_decay * carried + block_end, carried)  6.2 us
  transfers between devices with their start and end apart: 10, of which 8 were waited for; matrix products, arithmetic and copies ran while one was open for 42% of the time, Pallas kernels for 0%

commit v1 on v0

v1 whole, which is shorter than its diff:
```python
import functools

import jax
import jax.numpy as jnp
from jax import lax
from jax.experimental import pallas as pl
from jax.experimental.pallas import tpu as pltpu
from jax.sharding import PartitionSpec as P

LANES = 128
SEGS = 8
HALO = 16


def repeat(count, unroll, body, carry):
    whole = count // unroll

    def group(index, carried):
        for step in range(unroll):
            carried = body(index * unroll + step, carried)
        return carried

    carry = lax.fori_loop(0, whole, group, carry)
    for step in range(whole * unroll, count):
        carry = body(step, carry)
    return carry


def tree_sum(terms):
    terms = list(terms)
    while len(terms) > 1:
        terms = [
            terms[i] + terms[i + 1] if i + 1 < len(terms) else terms[i]
            for i in range(0, len(terms), 2)
        ]
    return terms[0]


def spread(row):
    return jnp.broadcast_to(row, (SEGS, LANES))


def relayout(natural, turned, first, count, length):
    def body(j, _):
        turned[j] = natural[pl.ds(first + j, SEGS, stride=length), :]
        return 0

    repeat(count, 8, body, 0)


def convolve(length, taps, w_ref, xt, ct, q_at, k_at, v_at, src, ups):
    weights = [[spread(w_ref[k, i : i + 1, :]) for i in range(taps)] for k in range(3)]

    def body(t, _):
        window = [xt[t + taps - 1 - i] for i in range(taps)]
        q, k, v = (tree_sum(weights[s][i] * window[i] for i in range(taps)) for s in range(3))
        if q_at is not None:
            q_at[t] = q
        if k_at is not None:
            k_at[t] = k
            v_at[t] = v
        src[t] = k * v
        ups[t] = q * ct[t]
        return 0

    repeat(length, 3, body, 0)


def local_states(length, poles, decay, src, ups, ends, heads):
    d = [spread(decay[p : p + 1, :]) for p in range(poles)]
    zero = jnp.zeros((SEGS, LANES), jnp.float32)

    def body(t, states):
        x, u = src[t], ups[length - 1 - t]
        return (
            tuple(d[p] * states[0][p] + x for p in range(poles)),
            tuple(d[p] * states[1][p] + u for p in range(poles)),
        )

    states = ((zero,) * poles, (zero,) * poles)
    short = length - SEGS
    states = repeat(short, 4, body, states)
    for p in range(poles):
        ends[1, p * SEGS : (p + 1) * SEGS, :] = states[0][p]
        heads[1, p * SEGS : (p + 1) * SEGS, :] = states[1][p]
    for t in range(SEGS):
        states = body(short + t, states)
    for p in range(poles):
        ends[0, p * SEGS : (p + 1) * SEGS, :] = states[0][p]
        heads[0, p * SEGS : (p + 1) * SEGS, :] = states[1][p]


def link_segments(length, poles, inverse, ends, heads, starts, nexts):
    over = jnp.exp(-float(length) * inverse)
    partial = jnp.exp(-float(length - SEGS) * inverse)
    carried = jnp.zeros_like(inverse)
    for s in range(SEGS):
        starts[s] = carried
        if s < SEGS - 1:
            carried = over * carried + ends[0, pl.ds(s, poles, stride=SEGS), :]
    total = partial * carried + ends[1, pl.ds(SEGS - 1, poles, stride=SEGS), :]
    carried = jnp.zeros_like(inverse)
    for s in reversed(range(SEGS)):
        nexts[s] = carried
        if s:
            carried = over * carried + heads[0, pl.ds(s, poles, stride=SEGS), :]
    return total, partial * carried + heads[1, pl.ds(0, poles, stride=SEGS), :]


def enter(length, poles, inverse, incoming, after, starts, nexts, begin, finish):
    for s in range(SEGS):
        begin[pl.ds(s, poles, stride=SEGS), :] = (
            starts[s] + jnp.exp(-float(s * length) * inverse) * incoming
        )
        finish[pl.ds(s, poles, stride=SEGS), :] = (
            nexts[s] + jnp.exp(-float((SEGS - 1 - s) * length) * inverse) * after
        )


def mix(length, poles, backward, decay, gain, skip, entering, stream, store):
    d = [spread(decay[p : p + 1, :]) for p in range(poles)]
    g = [spread(gain[p : p + 1, :]) for p in range(poles)]
    skip = spread(skip)
    states = tuple(entering[p * SEGS : (p + 1) * SEGS, :] for p in range(poles))

    def body(step, states):
        t = length - 1 - step if backward else step
        x = stream[t]
        states = tuple(d[p] * states[p] + x for p in range(poles))
        store(t, tree_sum([g[p] * states[p] for p in range(poles)] + [skip * x]))
        return states

    repeat(length, 4, body, states)


def gather_taps(length, taps, w_ref, streams, natural):
    weights = [[spread(w_ref[k, i : i + 1, :]) for i in range(taps)] for k in range(3)]
    for stream in streams:
        for j in range(taps - 1):
            stream[length + j] = pltpu.roll(stream[j], SEGS - 1, 0)

    def body(t, _):
        grad = tree_sum(
            tree_sum(weights[k][i] * streams[k][t + i] for i in range(taps)) for k in range(3)
        )
        natural[pl.ds(t, SEGS, stride=length), :] = grad
        return 0

    repeat(length, 3, body, 0)


def stage(rows, taps, before, tok, after, cot, cot_after, natural, cnat, xt, ct):
    length = rows // SEGS + 1
    natural[0:HALO, :] = before[...].astype(jnp.float32)
    natural[HALO : HALO + rows, :] = tok[...].astype(jnp.float32)
    natural[HALO + rows : HALO + rows + HALO, :] = after[...].astype(jnp.float32)
    cnat[0:rows, :] = cot[...].astype(jnp.float32)
    cnat[rows : rows + HALO, :] = cot_after[...].astype(jnp.float32)
    relayout(natural, xt, HALO - (taps - 1), length + taps - 1, length)
    relayout(cnat, ct, 0, length, length)


def first_kernel(rows, poles, taps, before, tok, after, cot, cot_after, w_ref, inv_ref,
                 starts, nexts, sums, natural, cnat, xt, ct, src, ups, decay, ends, heads):
    length = rows // SEGS + 1
    stage(rows, taps, before, tok, after, cot, cot_after, natural, cnat, xt, ct)
    convolve(length, taps, w_ref, xt, ct, None, None, None, src, ups)
    inverse = inv_ref[...]
    decay[...] = jnp.exp(-inverse)
    local_states(length, poles, decay, src, ups, ends, heads)
    total, head = link_segments(length, poles, inverse, ends, heads, starts, nexts)
    sums[0] = total
    sums[1] = head


def second_kernel(rows, poles, taps, before, tok, after, cot, cot_after, w_ref, inv_ref, gain, skip,
                  starts, nexts, entry, out, natural, cnat, xt, ct, k_at, v_at, src, ups, dq,
                  decay, begin, finish):
    length = rows // SEGS + 1
    stage(rows, taps, before, tok, after, cot, cot_after, natural, cnat, xt, ct)
    convolve(length, taps, w_ref, xt, ct, None, k_at, v_at, src, ups)
    inverse = inv_ref[...]
    decay[...] = jnp.exp(-inverse)
    enter(length, poles, inverse, entry[0], entry[1], starts, nexts, begin, finish)

    def store_q(t, value):
        dq[t] = ct[t] * value

    def store_kv(t, value):
        k, v = k_at[t], v_at[t]
        k_at[t] = value * v
        v_at[t] = value * k

    mix(length, poles, False, decay, gain, skip[...], begin, src, store_q)
    mix(length, poles, True, decay, gain, skip[...], finish, ups, store_kv)
    gather_taps(length, taps, w_ref, (dq, k_at, v_at), natural)
    out[...] = natural[0:rows, :].astype(jnp.bfloat16)


def shifted(block, axis, distance):
    devices = range(lax.axis_size(axis))
    route = [(i - distance, i) for i in devices if i - distance in devices]
    return lax.ppermute(block, axis, route)


def per_device(tokens, cotangent, conv_weight, residue, decay_length, skip_gain):
    tok = lax.all_to_all(tokens, "grp", split_axis=1, concat_axis=0, tiled=True)
    cot = lax.all_to_all(cotangent, "grp", split_axis=1, concat_axis=0, tiled=True)
    rows, chans = tok.shape
    poles, taps = residue.shape[0], conv_weight.shape[1]
    length = rows // SEGS + 1
    inverse = 1.0 / decay_length
    gain = residue * jnp.sqrt(-jnp.expm1(-2.0 * inverse))
    before = shifted(tok[rows - HALO :], "ctx", 1)
    behind = shifted(jnp.concatenate([tok[:HALO], cot[:HALO]], 0), "ctx", -1)
    after, cot_after = behind[:HALO], behind[HALO:]
    f32 = jnp.float32

    def cols(*lead):
        return pl.BlockSpec((*lead, LANES), lambda c: (0,) * len(lead) + (c,))

    def shape(*dims):
        return jax.ShapeDtypeStruct(dims, f32)

    def turned(extra=0):
        return pltpu.VMEM((length + extra, SEGS, LANES), f32)

    grid = (chans // LANES,)
    edge, whole = cols(HALO), cols(rows)
    base = [edge, whole, edge, whole, edge, cols(3, taps), cols(poles)]
    data = (before, tok, after, cot, cot_after, conv_weight, inverse)
    params = pltpu.CompilerParams(vmem_limit_bytes=56 * 2**20)
    natural = pltpu.VMEM((rows + 2 * HALO, LANES), f32)
    small = pltpu.VMEM((poles * SEGS, LANES), f32)
    starts, nexts, sums = pl.pallas_call(
        functools.partial(first_kernel, rows, poles, taps),
        grid=grid,
        out_shape=(shape(SEGS, poles, chans), shape(SEGS, poles, chans), shape(2, poles, chans)),
        in_specs=base,
        out_specs=(cols(SEGS, poles), cols(SEGS, poles), cols(2, poles)),
        scratch_shapes=[
            natural, natural, turned(taps - 1), turned(), turned(), turned(),
            pltpu.VMEM((poles, LANES), f32),
            pltpu.VMEM((2, poles * SEGS, LANES), f32),
            pltpu.VMEM((2, poles * SEGS, LANES), f32),
        ],
        compiler_params=params,
    )(*data)
    every = lax.all_gather(sums, "ctx")
    me = lax.axis_index("ctx")
    over = jnp.exp(-float(rows) * inverse)
    incoming = jnp.zeros_like(inverse)
    later = jnp.zeros_like(inverse)
    for j in range(lax.axis_size("ctx")):
        incoming = jnp.where(j < me, over * incoming + every[j, 0], incoming)
        r = lax.axis_size("ctx") - 1 - j
        later = jnp.where(r > me, over * later + every[r, 1], later)
    entry = jnp.stack([incoming, later])
    return pl.pallas_call(
        functools.partial(second_kernel, rows, poles, taps),
        grid=grid,
        out_shape=jax.ShapeDtypeStruct((rows, chans), jnp.bfloat16),
        in_specs=base + [cols(poles), cols(1), cols(SEGS, poles), cols(SEGS, poles), cols(2, poles)],
        out_specs=whole,
        scratch_shapes=[
            natural, natural, turned(taps - 1), turned(),
            turned(taps - 1), turned(taps - 1), turned(), turned(), turned(taps - 1),
            pltpu.VMEM((poles, LANES), f32), small, small,
        ],
        compiler_params=params,
    )(*data, gain, skip_gain[None], starts, nexts, entry)


def solution(mesh):
    placed = (
        P(("ctx", "grp"), None),
        P(("ctx", "grp"), None),
        P(None, None, "grp"),
        P(None, "grp"),
        P(None, "grp"),
        P("grp"),
    )
    return jax.shard_map(
        per_device, mesh=mesh, in_specs=placed, out_specs=P("ctx", "grp"), check_vma=False
    )
```

time: 276 us -> 116 us (0.42)
  the two profiles are of different devices: /device:TPU:27 before, /device:TPU:0 now
where the time goes in v1:
time: 116 us; the launch traced here: 115 us
  waiting for transfers between devices  50.8 us (44%)
  Pallas kernels  34.9 us (30%)
  starting transfers between devices  15.3 us (13%)
  blocking collectives  7.81 us (7%)
  local copies, waits for them, and re-layouts  4.62 us (4%)
  other arithmetic  1.9 us (2%)
    all_to_all x1, waiting for transfers between devices, per_device(): lax.all_to_all(cotangent, 'grp', split_axis=1, concat_axis=0, tiled=True)  25.9 us
    all_to_all x1, waiting for transfers between devices, per_device(): tok = lax.all_to_all(tokens, 'grp', split_axis=1, concat_axis=0, tiled=True)  24.7 us
    pallas_call x1, Pallas kernels, per_device(): pl.pallas_call(functools.partial(second_kernel, rows, poles, taps), grid=...  22.6 us
    pallas_call x1, Pallas kernels, per_device(): pl.pallas_call(functools.partial(first_kernel, rows, poles, taps), grid=g...  12.2 us
    all_gather x1, blocking collectives, per_device(): every = lax.all_gather(sums, 'ctx')  7.81 us
    all_to_all x1, starting transfers between devices, per_device(): tok = lax.all_to_all(tokens, 'grp', split_axis=1, concat_axis=0, tiled=True)  7.38 us
    ppermute x2, starting transfers between devices, shifted(): return lax.ppermute(block, axis, route)  4.31 us
    all_to_all x1, starting transfers between devices, per_device(): lax.all_to_all(cotangent, 'grp', split_axis=1, concat_axis=0, tiled=True)  3.59 us
  transfers between devices with their start and end apart: 4, of which 3 were waited for; matrix products, arithmetic and copies ran while one was open for 2% of the time, Pallas kernels for 0%

profile of v1, /device:TPU:0, one launch (start us, length us, event | category | flops | bytes accessed | tf_op | source)
XLA Modules:
  0.0 115.3 jit_solution(12881385832950902171)
XLA Ops:
  0.0 2.3 %copy.16 = bf16[16,8,8,512]{3,2,0,1:T(8,128)(2,1)} copy(bf16[16,8,8,512]{3,2,1,0:T(8,128)(2,1)} %bitcast.91) | data formatting | bytes 2097152 | tf_op jit(solution)/shard_map/all_to_all | solution.py:207
  2.3 0.0 copy-start.2
  2.3 7.4 %all-to-all-start = ((bf16[128,8,512]{2,0,1:T(8,128)(2,1)}), bf16[128,8,512]{2,0,1:T(8,128)(2,1)S(1)}, u32[]{:S(2)}, u32[]{:S(2)}) async-start(bf16[128,8,512]{2,0,1:T(8,128)(2,1)} %bitcast.83), calls=%async_computation | async-start | bytes 2097152 | tf_op jit(solution)/shard_map/all_to_all | solution.py:207
  9.7 0.0 copy-done.2
  9.7 1.1 copy.15
  10.8 24.7 %all-to-all-done = bf16[128,8,512]{2,0,1:T(8,128)(2,1)S(1)} async-done(((bf16[128,8,512]{2,0,1:T(8,128)(2,1)}), bf16[128,8,512]{2,0,1:T(8,128)(2,1)S(1)}, u32[]{:S(2)}, u32[]{:S(2)}) %all-to-all-start) | async-done | bytes 1048608 | tf_op jit(solution)/shard_map/all_to_all | solution.py:207
  35.4 0.0 copy-start
  35.5 3.6 %all-to-all-start.1 = ((bf16[128,8,512]{2,0,1:T(8,128)(2,1)}), bf16[128,8,512]{2,0,1:T(8,128)(2,1)S(1)}, u32[]{:S(2)}, u32[]{:S(2)}) async-start(bf16[128,8,512]{2,0,1:T(8,128)(2,1)} %bitcast.82), calls=%async_computation.1 | async-start | bytes 2097152 | tf_op jit(solution)/shard_map/all_to_all | solution.py:208
  39.0 0.0 copy-done
  39.1 25.9 %all-to-all-done.1 = bf16[128,8,512]{2,0,1:T(8,128)(2,1)S(1)} async-done(((bf16[128,8,512]{2,0,1:T(8,128)(2,1)}), bf16[128,8,512]{2,0,1:T(8,128)(2,1)S(1)}, u32[]{:S(2)}, u32[]{:S(2)}) %all-to-all-start.1) | async-done | bytes 1048608 | tf_op jit(solution)/shard_map/all_to_all | solution.py:208
  65.0 0.0 copy-start.1
  65.0 0.0 copy-start.3
  65.0 1.3 %collective-permute-start.1 = (bf16[32,512]{1,0:T(8,128)(2,1)S(1)}, bf16[32,512]{1,0:T(8,128)(2,1)S(1)}, u32[]{:S(2)}, u32[]{:S(2)}) collective-permute-start(bf16[32,512]{1,0:T(8,128)(2,1)S(1)} %pad_maximum_fusion.1), channel_id=1, source_target_pairs={{8,0},{16,8},{24,16},{9,1},{17,9},{25,17},{10,2},{18,10},{26,18},{... | collective-permute-start | bytes 98312 | tf_op jit(solution)/shard_map/ppermute | solution.py:203
  66.3 0.0 copy-done.3
  66.3 0.6 broadcast_divide_fusion.inv_ref
  66.9 3.0 %collective-permute-start = (bf16[16,512]{1,0:T(8,128)(2,1)S(1)}, bf16[16,512]{1,0:T(8,128)(2,1)S(1)}, u32[]{:S(2)}, u32[]{:S(2)}) collective-permute-start(bf16[16,512]{1,0:T(8,128)(2,1)S(1)} %get-tuple-element.12), channel_id=1, source_target_pairs={{0,8},{8,16},{16,24},{1,9},{9,17},{17,25},{2,10},{10,18},{18,26},{... | collective-permute-start | bytes 49160 | tf_op jit(solution)/shard_map/ppermute | solution.py:203
  70.0 0.0 collective-permute-done.1
  70.0 0.6 fusion.19
  70.6 0.2 collective-permute-done.before
  70.8 0.0 copy-start.4
  70.8 0.0 copy-done.1
  70.8 0.6 copy-done.4
  71.4 12.2 %shard_map.64 = (f32[8,16,512]{2,1,0:T(8,128)}, f32[8,16,512]{2,1,0:T(8,128)}, f32[2,16,512]{2,1,0:T(8,128)}) custom-call(bf16[16,512]{1,0:T(8,128)(2,1)} %copy-done.4, bf16[1024,512]{1,0:T(8,128)(2,1)} %bitcast.85, bf16[16,512]{1,0:T(8,128)(2,1)} %get-tuple-element.17.after, bf16[1024,512]{1,0:T(8,128)(2,1)} %bitcast.88, ...), custom_call_target="tpu_custom_call" | custom-call | tf_op jit(solution)/shard_map/pallas_call | solution.py:235
  83.6 0.0 copy-start.5
  83.6 7.8 %all-gather = f32[8,16,512]{2,1,0:T(8,128)S(1)} all-gather(f32[2,16,512]{2,1,0:T(8,128)} %get-tuple-element.10), channel_id=2, replica_groups=mesh['ctx'=4,'grp'=8] {'ctx'}, dimensions={0}, use_global_device_ids=true | all-gather | bytes 327680 | tf_op jit(solution)/shard_map/all_gather | solution.py:249
  91.4 0.0 copy-done.5
  91.4 0.7 fusion.11
  92.1 0.6 pad_maximum_fusion.entry
  92.7 22.6 %shard_map.65 = bf16[1024,512]{1,0:T(8,128)(2,1)} custom-call(bf16[16,512]{1,0:T(8,128)(2,1)} %copy-done.4, bf16[1024,512]{1,0:T(8,128)(2,1)} %bitcast.86, bf16[16,512]{1,0:T(8,128)(2,1)} %get-tuple-element.17.after, bf16[1024,512]{1,0:T(8,128)(2,1)} %bitcast.89, bf16[16,512]{1,0:T(8,128)(2,1)} %get-tuple-element.16.cot_after, f32[3,7,512]{2,1,0:T(8,128)} %w_ref.3, ...), custom_call_target="tpu_custom_call" | custom-call | tf_op jit(solution)/shard_map/pallas_call | solution.py:259
  (3 shorter events, 0.0 us)
Async XLA Ops:
  2.3 7.4 %copy-start.2 = (bf16[128,4096]{1,0:T(8,128)(2,1)S(1)}, bf16[128,4096]{1,0:T(8,128)(2,1)}, u32[]{:S(2)}) copy-start(bf16[128,4096]{1,0:T(8,128)(2,1)} %param.7) | copy-start | bytes 3145732
  2.3 33.2 %all-to-all-start = ((bf16[128,8,512]{2,0,1:T(8,128)(2,1)}), bf16[128,8,512]{2,0,1:T(8,128)(2,1)S(1)}, u32[]{:S(2)}, u32[]{:S(2)}) async-start(bf16[128,8,512]{2,0,1:T(8,128)(2,1)} %bitcast.83), calls=%async_computation | async-start | bytes 2097152 | tf_op jit(solution)/shard_map/all_to_all | solution.py:207
  35.4 3.6 %copy-start = (bf16[128,8,512]{2,0,1:T(8,128)(2,1)}, bf16[128,8,512]{2,0,1:T(8,128)(2,1)S(1)}, u32[]{:S(2)}) copy-start(bf16[128,8,512]{2,0,1:T(8,128)(2,1)S(1)} %all-to-all-done) | copy-start | bytes 3145732
  35.5 29.5 %all-to-all-start.1 = ((bf16[128,8,512]{2,0,1:T(8,128)(2,1)}), bf16[128,8,512]{2,0,1:T(8,128)(2,1)S(1)}, u32[]{:S(2)}, u32[]{:S(2)}) async-start(bf16[128,8,512]{2,0,1:T(8,128)(2,1)} %bitcast.82), calls=%async_computation.1 | async-start | bytes 2097152 | tf_op jit(solution)/shard_map/all_to_all | solution.py:208
  65.0 5.8 %copy-start.1 = (bf16[128,8,512]{2,0,1:T(8,128)(2,1)}, bf16[128,8,512]{2,0,1:T(8,128)(2,1)S(1)}, u32[]{:S(2)}) copy-start(bf16[128,8,512]{2,0,1:T(8,128)(2,1)S(1)} %all-to-all-done.1) | copy-start | bytes 3145732
  65.0 1.3 %copy-start.3 = (f32[16,512]{1,0:T(8,128)S(1)}, f32[16,512]{1,0:T(8,128)}, u32[]{:S(2)}) copy-start(f32[16,512]{1,0:T(8,128)} %param.10) | copy-start | bytes 98308
  65.0 5.0 %collective-permute-start.1 = (bf16[32,512]{1,0:T(8,128)(2,1)S(1)}, bf16[32,512]{1,0:T(8,128)(2,1)S(1)}, u32[]{:S(2)}, u32[]{:S(2)}) collective-permute-start(bf16[32,512]{1,0:T(8,128)(2,1)S(1)} %pad_maximum_fusion.1), channel_id=1, source_target_pairs={{8,0},{16,8},{24,16},{9,1},{17,9},{25,17},{10,2},{18,10},{26,18},{... | collective-permute-start | bytes 98312 | tf_op jit(solution)/shard_map/ppermute | solution.py:203
  66.9 3.8 %collective-permute-start = (bf16[16,512]{1,0:T(8,128)(2,1)S(1)}, bf16[16,512]{1,0:T(8,128)(2,1)S(1)}, u32[]{:S(2)}, u32[]{:S(2)}) collective-permute-start(bf16[16,512]{1,0:T(8,128)(2,1)S(1)} %get-tuple-element.12), channel_id=1, source_target_pairs={{0,8},{8,16},{16,24},{1,9},{9,17},{17,25},{2,10},{10,18},{18,26},{... | collective-permute-start | bytes 49160 | tf_op jit(solution)/shard_map/ppermute | solution.py:203
  70.8 0.6 copy-start.4
  83.6 7.8 %copy-start.5 = (f32[16,512]{1,0:T(8,128)S(1)}, f32[16,512]{1,0:T(8,128)}, u32[]{:S(2)}) copy-start(f32[16,512]{1,0:T(8,128)} %param.9) | copy-start | bytes 98308

commit v2 on v1

v2 whole, which is shorter than its diff:
```python
import functools

import jax
import jax.numpy as jnp
from jax import lax
from jax.experimental import pallas as pl
from jax.experimental.pallas import tpu as pltpu
from jax.sharding import PartitionSpec as P

MESH = pl.DeviceIdType.MESH
LANES = 128
SEGS = 8
HALO = 16


def repeat(count, unroll, body, carry):
    whole = count // unroll

    def group(index, carried):
        for step in range(unroll):
            carried = body(index * unroll + step, carried)
        return carried

    carry = lax.fori_loop(0, whole, group, carry)
    for step in range(whole * unroll, count):
        carry = body(step, carry)
    return carry


def tree_sum(terms):
    terms = list(terms)
    while len(terms) > 1:
        terms = [
            terms[i] + terms[i + 1] if i + 1 < len(terms) else terms[i]
            for i in range(0, len(terms), 2)
        ]
    return terms[0]


def spread(row):
    return jnp.broadcast_to(row, (SEGS, LANES))


def relayout(natural, turned, first, count, length):
    def body(j, _):
        turned[j] = natural[pl.ds(first + j, SEGS, stride=length), :]
        return 0

    repeat(count, 8, body, 0)


def convolve(length, taps, w_ref, xt, ct, q_at, k_at, v_at, src, ups):
    weights = [[spread(w_ref[k, i : i + 1, :]) for i in range(taps)] for k in range(3)]

    def body(t, _):
        window = [xt[t + taps - 1 - i] for i in range(taps)]
        q, k, v = (tree_sum(weights[s][i] * window[i] for i in range(taps)) for s in range(3))
        if q_at is not None:
            q_at[t] = q
        if k_at is not None:
            k_at[t] = k
            v_at[t] = v
        src[t] = k * v
        ups[t] = q * ct[t]
        return 0

    repeat(length, 3, body, 0)


def local_states(length, poles, decay, src, ups, ends, heads):
    d = [spread(decay[p : p + 1, :]) for p in range(poles)]
    zero = jnp.zeros((SEGS, LANES), jnp.float32)

    def body(t, states):
        x, u = src[t], ups[length - 1 - t]
        return (
            tuple(d[p] * states[0][p] + x for p in range(poles)),
            tuple(d[p] * states[1][p] + u for p in range(poles)),
        )

    states = ((zero,) * poles, (zero,) * poles)
    short = length - SEGS
    states = repeat(short, 4, body, states)
    for p in range(poles):
        ends[1, p * SEGS : (p + 1) * SEGS, :] = states[0][p]
        heads[1, p * SEGS : (p + 1) * SEGS, :] = states[1][p]
    for t in range(SEGS):
        states = body(short + t, states)
    for p in range(poles):
        ends[0, p * SEGS : (p + 1) * SEGS, :] = states[0][p]
        heads[0, p * SEGS : (p + 1) * SEGS, :] = states[1][p]


def link_segments(length, poles, inverse, ends, heads, starts, nexts):
    over = jnp.exp(-float(length) * inverse)
    partial = jnp.exp(-float(length - SEGS) * inverse)
    carried = jnp.zeros_like(inverse)
    for s in range(SEGS):
        starts[s] = carried
        if s < SEGS - 1:
            carried = over * carried + ends[0, pl.ds(s, poles, stride=SEGS), :]
    total = partial * carried + ends[1, pl.ds(SEGS - 1, poles, stride=SEGS), :]
    carried = jnp.zeros_like(inverse)
    for s in reversed(range(SEGS)):
        nexts[s] = carried
        if s:
            carried = over * carried + heads[0, pl.ds(s, poles, stride=SEGS), :]
    return total, partial * carried + heads[1, pl.ds(0, poles, stride=SEGS), :]


def enter(length, poles, inverse, incoming, after, starts, nexts, begin, finish):
    for s in range(SEGS):
        begin[pl.ds(s, poles, stride=SEGS), :] = (
            starts[s] + jnp.exp(-float(s * length) * inverse) * incoming
        )
        finish[pl.ds(s, poles, stride=SEGS), :] = (
            nexts[s] + jnp.exp(-float((SEGS - 1 - s) * length) * inverse) * after
        )


def mix(length, poles, backward, decay, gain, skip, entering, stream, store):
    d = [spread(decay[p : p + 1, :]) for p in range(poles)]
    g = [spread(gain[p : p + 1, :]) for p in range(poles)]
    skip = spread(skip)
    states = tuple(entering[p * SEGS : (p + 1) * SEGS, :] for p in range(poles))

    def body(step, states):
        t = length - 1 - step if backward else step
        x = stream[t]
        states = tuple(d[p] * states[p] + x for p in range(poles))
        store(t, tree_sum([g[p] * states[p] for p in range(poles)] + [skip * x]))
        return states

    repeat(length, 4, body, states)


def gather_taps(length, taps, w_ref, streams, natural):
    weights = [[spread(w_ref[k, i : i + 1, :]) for i in range(taps)] for k in range(3)]
    for stream in streams:
        for j in range(taps - 1):
            stream[length + j] = pltpu.roll(stream[j], SEGS - 1, 0)

    def body(t, _):
        grad = tree_sum(
            tree_sum(weights[k][i] * streams[k][t + i] for i in range(taps)) for k in range(3)
        )
        natural[pl.ds(t, SEGS, stride=length), :] = grad
        return 0

    repeat(length, 3, body, 0)


def stage(rows, taps, before, tok, after, cot, cot_after, natural, cnat, xt, ct):
    length = rows // SEGS + 1
    natural[0:HALO, :] = before.astype(jnp.float32)
    natural[HALO : HALO + rows, :] = tok.astype(jnp.float32)
    natural[HALO + rows : HALO + rows + HALO, :] = after.astype(jnp.float32)
    cnat[0:rows, :] = cot.astype(jnp.float32)
    cnat[rows : rows + HALO, :] = cot_after.astype(jnp.float32)
    relayout(natural, xt, HALO - (taps - 1), length + taps - 1, length)
    relayout(cnat, ct, 0, length, length)


def kernel(ctxs, grps, poles, taps, tokens, cotangent, w_ref, inv_ref, gain_ref, skip_ref, out,
           tok_in, cot_in, before, after, cot_after, every,
           natural, cnat, xt, ct, k_at, v_at, src, ups, dq,
           decay, weights, gain, ends, heads, starts, nexts, begin, finish,
           send_sem, recv_sem, edge_send, edge_recv, state_send, state_recv):
    ctx, grp = lax.axis_index("ctx"), lax.axis_index("grp")
    share, chans = tokens.shape[0], out.shape[1]
    rows = share * grps
    length = rows // SEGS + 1
    chunks = chans // LANES
    first, last = ctx == 0, ctx == ctxs - 1
    lead, tail = grp == 0, grp == grps - 1

    barrier = pltpu.get_barrier_semaphore()

    def greet(to_ctx, to_grp):
        pl.semaphore_signal(barrier, inc=1, device_id=(to_ctx, to_grp), device_id_type=MESH)

    for off in range(1, grps):
        greet(ctx, lax.rem(grp + off, grps))
    for off in range(1, ctxs):
        greet(lax.rem(ctx + off, ctxs), grp)

    @pl.when(ctx > 0)
    def _():
        greet(ctx - 1, grps - 1)

    @pl.when(ctx < ctxs - 1)
    def _():
        greet(ctx + 1, 0)

    sends_tail = jnp.logical_and(tail, ctx < ctxs - 1)
    sends_lead = jnp.logical_and(lead, ctx > 0)
    edges = jnp.where(sends_tail, grps, 0) + jnp.where(sends_lead, grps, 0)
    pl.semaphore_wait(barrier, grps - 1 + ctxs - 1 + edges)

    def edge_copy(kind, j):
        source = (tokens, tokens, cotangent)[kind]
        row = share - HALO if kind == 0 else 0
        return pltpu.make_async_remote_copy(
            src_ref=source.at[row : row + HALO, pl.ds(pl.multiple_of(j * chans, LANES), chans)],
            dst_ref=(before, after, cot_after)[kind],
            send_sem=edge_send.at[kind, j],
            recv_sem=edge_recv.at[kind],
            device_id=(ctx + 1 if kind == 0 else ctx - 1, j),
            device_id_type=MESH,
        )

    @pl.when(sends_tail)
    def _():
        for j in range(grps):
            edge_copy(0, j).start()

    @pl.when(sends_lead)
    def _():
        for j in range(grps):
            edge_copy(1, j).start()
            edge_copy(2, j).start()

    def columns(owner, c):
        return pl.ds(pl.multiple_of(owner * chans + c * LANES, LANES), LANES)

    def block_rows(owner):
        return pl.ds(pl.multiple_of(owner * share, share), share)

    def own_copy(a, c):
        source, target = ((tokens, tok_in), (cotangent, cot_in))[a]
        return pltpu.make_async_copy(
            source.at[:, columns(grp, c)], target.at[c, block_rows(grp), :], recv_sem.at[a, c, grp]
        )

    def block_copy(a, c, sender, receiver):
        source, target = ((tokens, tok_in), (cotangent, cot_in))[a]
        return pltpu.make_async_remote_copy(
            src_ref=source.at[:, columns(receiver, c)],
            dst_ref=target.at[c, block_rows(sender), :],
            send_sem=send_sem.at[a, c, receiver],
            recv_sem=recv_sem.at[a, c, sender],
            device_id=(ctx, receiver),
            device_id_type=MESH,
        )

    def send_chunk(c, _):
        for a in range(2):
            own_copy(a, c).start()
            for off in range(1, grps):
                block_copy(a, c, grp, lax.rem(grp + off, grps)).start()
        return 0

    lax.fori_loop(0, chunks, send_chunk, 0)

    @pl.when(first)
    def _():
        before[...] = jnp.zeros_like(before)

    @pl.when(last)
    def _():
        after[...] = jnp.zeros_like(after)
        cot_after[...] = jnp.zeros_like(cot_after)

    @pl.when(ctx > 0)
    def _():
        edge_copy(0, 0).wait_recv()

    @pl.when(ctx < ctxs - 1)
    def _():
        edge_copy(1, 0).wait_recv()
        edge_copy(2, 0).wait_recv()

    def state_copy(c, sender, receiver):
        return pltpu.make_async_remote_copy(
            src_ref=every.at[c, sender],
            dst_ref=every.at[c, sender],
            send_sem=state_send.at[c, receiver],
            recv_sem=state_recv.at[c, sender],
            device_id=(receiver, grp),
            device_id_type=MESH,
        )

    def here(c):
        return pl.ds(pl.multiple_of(c * LANES, LANES), LANES)

    def phase_one(c):
        slot = lax.rem(c, 2)
        for a in range(2):
            own_copy(a, c).wait()
            for off in range(1, grps):
                sender = lax.rem(grp + off, grps)
                block_copy(a, c, sender, sender).wait_recv()
        at = here(c)
        stage(rows, taps, before[:, at], tok_in[c], after[:, at], cot_in[c], cot_after[:, at],
              natural, cnat, xt, ct.at[slot])
        weights[...] = w_ref[:, :, at]
        convolve(length, taps, weights, xt, ct.at[slot], None, k_at.at[slot], v_at.at[slot],
                 src.at[slot], ups.at[slot])
        inverse = inv_ref[:, at]
        decay[...] = jnp.exp(-inverse)
        local_states(length, poles, decay, src.at[slot], ups.at[slot], ends, heads)
        total, head = link_segments(
            length, poles, inverse, ends, heads, starts.at[slot], nexts.at[slot]
        )
        every[c, ctx, 0] = total
        every[c, ctx, 1] = head
        for off in range(1, ctxs):
            state_copy(c, ctx, lax.rem(ctx + off, ctxs)).start()

    def phase_two(c):
        slot = lax.rem(c, 2)
        for off in range(1, ctxs):
            sender = lax.rem(ctx + off, ctxs)
            state_copy(c, sender, sender).wait_recv()
        at = here(c)
        weights[...] = w_ref[:, :, at]
        inverse = inv_ref[:, at]
        decay[...] = jnp.exp(-inverse)
        gain[...] = gain_ref[:, at]
        skip = skip_ref[:, at]
        over = jnp.exp(-float(rows) * inverse)
        incoming = jnp.zeros_like(inverse)
        later = jnp.zeros_like(inverse)
        for j in range(ctxs):
            incoming = jnp.where(j < ctx, over * incoming + every[c, j, 0], incoming)
            r = ctxs - 1 - j
            later = jnp.where(r > ctx, over * later + every[c, r, 1], later)
        enter(length, poles, inverse, incoming, later, starts.at[slot], nexts.at[slot], begin, finish)
        k_here, v_here, c_here = k_at.at[slot], v_at.at[slot], ct.at[slot]

        def store_q(t, value):
            dq[t] = c_here[t] * value

        def store_kv(t, value):
            k, v = k_here[t], v_here[t]
            k_here[t] = value * v
            v_here[t] = value * k

        mix(length, poles, False, decay, gain, skip, begin, src.at[slot], store_q)
        mix(length, poles, True, decay, gain, skip, finish, ups.at[slot], store_kv)
        gather_taps(length, taps, weights, (dq, k_here, v_here), natural)
        out[:, at] = natural[0:rows, :].astype(jnp.bfloat16)

    phase_one(0)

    def stagger(c, _):
        phase_one(c)
        phase_two(c - 1)
        return 0

    lax.fori_loop(1, chunks, stagger, 0)
    phase_two(chunks - 1)

    def drain(c, _):
        for a in range(2):
            for off in range(1, grps):
                block_copy(a, c, grp, lax.rem(grp + off, grps)).wait_send()
        for off in range(1, ctxs):
            state_copy(c, ctx, lax.rem(ctx + off, ctxs)).wait_send()
        return 0

    lax.fori_loop(0, chunks, drain, 0)

    @pl.when(sends_tail)
    def _():
        for j in range(grps):
            edge_copy(0, j).wait_send()

    @pl.when(sends_lead)
    def _():
        for j in range(grps):
            edge_copy(1, j).wait_send()
            edge_copy(2, j).wait_send()


def per_device(tokens, cotangent, conv_weight, residue, decay_length, skip_gain):
    ctxs, grps = lax.axis_size("ctx"), lax.axis_size("grp")
    poles, chans = residue.shape
    taps = conv_weight.shape[1]
    rows = tokens.shape[0] * grps
    length = rows // SEGS + 1
    chunks = chans // LANES
    inverse = 1.0 / decay_length
    gain = residue * jnp.sqrt(-jnp.expm1(-2.0 * inverse))
    f32, bf16 = jnp.float32, jnp.bfloat16

    def turned(*lead, extra=0):
        return pltpu.VMEM((*lead, length + extra, SEGS, LANES), f32)

    more = taps - 1
    vmem = pl.BlockSpec(memory_space=pltpu.VMEM)
    far = pl.BlockSpec(memory_space=pl.ANY)
    small = pltpu.VMEM((poles * SEGS, LANES), f32)
    pair = pltpu.VMEM((2, poles * SEGS, LANES), f32)
    linked = pltpu.VMEM((2, SEGS, poles, LANES), f32)
    edge = pltpu.VMEM((HALO, chans), bf16)
    arrived = pltpu.VMEM((chunks, rows, LANES), bf16)
    natural = pltpu.VMEM((rows + 2 * HALO, LANES), f32)
    dma = pltpu.SemaphoreType.DMA
    return pl.pallas_call(
        functools.partial(kernel, ctxs, grps, poles, taps),
        out_shape=jax.ShapeDtypeStruct((rows, chans), bf16),
        in_specs=[far, far, vmem, vmem, vmem, vmem],
        out_specs=vmem,
        scratch_shapes=[
            arrived, arrived, edge, edge, edge, pltpu.VMEM((chunks, ctxs, 2, poles, LANES), f32),
            natural, natural, turned(extra=more), turned(2),
            turned(2, extra=more), turned(2, extra=more), turned(2), turned(2), turned(extra=more),
            pltpu.VMEM((poles, LANES), f32), pltpu.VMEM((3, taps, LANES), f32),
            pltpu.VMEM((poles, LANES), f32), pair, pair, linked, linked, small, small,
            dma((2, chunks, grps)), dma((2, chunks, grps)), dma((3, grps)), dma((3,)),
            dma((chunks, ctxs)), dma((chunks, ctxs)),
        ],
        compiler_params=pltpu.CompilerParams(
            vmem_limit_bytes=56 * 2**20, collective_id=0, has_side_effects=True
        ),
    )(tokens, cotangent, conv_weight, inverse, gain, skip_gain[None])


def solution(mesh):
    placed = (
        P(("ctx", "grp"), None),
        P(("ctx", "grp"), None),
        P(None, None, "grp"),
        P(None, "grp"),
        P(None, "grp"),
        P("grp"),
    )
    return jax.shard_map(
        per_device, mesh=mesh, in_specs=placed, out_specs=P("ctx", "grp"), check_vma=False
    )
```

time: 116 us -> 72.7 us (0.63)
  the two profiles are of different devices: /device:TPU:0 before, /device:TPU:27 now
where the time goes in v2:
time: 72.7 us; the launch traced here: 72 us
  Pallas kernels  68.3 us (94%)
  local copies, waits for them, and re-layouts  2.26 us (3%)
  other arithmetic  1.42 us (2%)
    pallas_call x1, Pallas kernels, per_device(): pl.pallas_call(functools.partial(kernel, ctxs, grps, poles, taps), out_sh...  68.3 us
    unnamed x1, local copies, waits for them, and re-layouts  2.26 us

profile of v2, /device:TPU:27, one launch (start us, length us, event | category | flops | bytes accessed | tf_op | source)
XLA Modules:
  0.0 72.0 jit_solution(11481524122088144504)
XLA Ops:
  0.0 1.4 %sqrt_multiply_fusion = (f32[16,512]{1,0:T(8,128)}, f32[16,512]{1,0:T(8,128)}) fusion(f32[16,512]{1,0:T(8,128)} %param.9, f32[16,512]{1,0:T(8,128)} %param.10), kind=kLoop, calls=%fused_computation | loop fusion | flops 32768 | bytes 131072 | tf_op jit(solution)/shard_map/mul | solution.py:384
  1.4 68.3 %shard_map.64 = bf16[1024,512]{1,0:T(8,128)(2,1)} custom-call(bf16[128,4096]{1,0:T(8,128)(2,1)} %tokens.1, bf16[128,4096]{1,0:T(8,128)(2,1)} %cotangent.1, f32[3,7,512]{2,1,0:T(8,128)} %w_ref.1, f32[16,512]{1,0:T(8,128)} %get-tuple-element.6.inv_ref, f32[16,512]{1,0:T(8,128)} %get-tuple-element.5.gain_ref, f32[1,512]{1,0:T(1,128)} %bitcast.1), custom_call_target="tpu_custom_call" | custom-call | tf_op jit(solution)/shard_map/pallas_call | solution.py:400
  69.8 2.3 %copy.8 = bf16[1024,512]{1,0:T(8,128)(2,1)} copy(bf16[1024,512]{1,0:T(8,128)(2,1)} %shard_map.64) | data formatting | bytes 2097152

commit v3 on v2

--- a/solution.py
+++ b/solution.py
@@ -250,7 +250,7 @@
                 block_copy(a, c, grp, lax.rem(grp + off, grps)).start()
         return 0
 
-    lax.fori_loop(0, chunks, send_chunk, 0)
+    lax.fori_loop(0, min(2, chunks), send_chunk, 0)
 
     @pl.when(first)
     def _():
@@ -306,6 +306,10 @@
         every[c, ctx, 1] = head
         for off in range(1, ctxs):
             state_copy(c, ctx, lax.rem(ctx + off, ctxs)).start()
+
+        @pl.when(c + 2 < chunks)
+        def _():
+            send_chunk(c + 2, 0)
 
     def phase_two(c):
         slot = lax.rem(c, 2)
@@ -341,7 +345,7 @@
         gather_taps(length, taps, weights, (dq, k_here, v_here), natural)
         out[:, at] = natural[0:rows, :].astype(jnp.bfloat16)
 
-    phase_one(0)
+    phase_one(jnp.int32(0))
 
     def stagger(c, _):
         phase_one(c)
@@ -349,7 +353,7 @@
         return 0
 
     lax.fori_loop(1, chunks, stagger, 0)
-    phase_two(chunks - 1)
+    phase_two(jnp.int32(chunks - 1))
 
     def drain(c, _):
         for a in range(2):

time: 72.7 us -> 72.7 us (level)
  no operation moved by 1% of the time
where the time goes in v3:
time: 72.7 us; the launch traced here: 72 us
  Pallas kernels  68.3 us (94%)
  local copies, waits for them, and re-layouts  2.26 us (3%)
  other arithmetic  1.42 us (2%)
    pallas_call x1, Pallas kernels, per_device(): pl.pallas_call(functools.partial(kernel, ctxs, grps, poles, taps), out_sh...  68.3 us
    unnamed x1, local copies, waits for them, and re-layouts  2.26 us

profile of v3, /device:TPU:27, one launch (start us, length us, event | category | flops | bytes accessed | tf_op | source)
XLA Modules:
  0.0 72.0 jit_solution(16192540347170373952)
XLA Ops:
  0.0 1.4 %sqrt_multiply_fusion = (f32[16,512]{1,0:T(8,128)}, f32[16,512]{1,0:T(8,128)}) fusion(f32[16,512]{1,0:T(8,128)} %param.9, f32[16,512]{1,0:T(8,128)} %param.10), kind=kLoop, calls=%fused_computation | loop fusion | flops 32768 | bytes 131072 | tf_op jit(solution)/shard_map/mul | solution.py:388
  1.4 68.3 %shard_map.64 = bf16[1024,512]{1,0:T(8,128)(2,1)} custom-call(bf16[128,4096]{1,0:T(8,128)(2,1)} %tokens.1, bf16[128,4096]{1,0:T(8,128)(2,1)} %cotangent.1, f32[3,7,512]{2,1,0:T(8,128)} %w_ref.1, f32[16,512]{1,0:T(8,128)} %get-tuple-element.6.inv_ref, f32[16,512]{1,0:T(8,128)} %get-tuple-element.5.gain_ref, f32[1,512]{1,0:T(1,128)} %bitcast.1), custom_call_target="tpu_custom_call" | custom-call | tf_op jit(solution)/shard_map/pallas_call | solution.py:404
  69.8 2.3 %copy.8 = bf16[1024,512]{1,0:T(8,128)(2,1)} copy(bf16[1024,512]{1,0:T(8,128)(2,1)} %shard_map.64) | data formatting | bytes 2097152

commit v4 on v2

--- a/solution.py
+++ b/solution.py
@@ -49,72 +49,54 @@
     repeat(count, 8, body, 0)
 
 
-def convolve(length, taps, w_ref, xt, ct, q_at, k_at, v_at, src, ups):
+def convolve(length, taps, w_ref, xt, q_at, k_at, v_at, src):
     weights = [[spread(w_ref[k, i : i + 1, :]) for i in range(taps)] for k in range(3)]
 
     def body(t, _):
         window = [xt[t + taps - 1 - i] for i in range(taps)]
         q, k, v = (tree_sum(weights[s][i] * window[i] for i in range(taps)) for s in range(3))
-        if q_at is not None:
-            q_at[t] = q
-        if k_at is not None:
-            k_at[t] = k
-            v_at[t] = v
+        q_at[t] = q
+        k_at[t] = k
+        v_at[t] = v
         src[t] = k * v
-        ups[t] = q * ct[t]
         return 0
 
     repeat(length, 3, body, 0)
 
 
-def local_states(length, poles, decay, src, ups, ends, heads):
+def local_states(length, poles, decay, fetch, ends):
     d = [spread(decay[p : p + 1, :]) for p in range(poles)]
     zero = jnp.zeros((SEGS, LANES), jnp.float32)
 
-    def body(t, states):
-        x, u = src[t], ups[length - 1 - t]
-        return (
-            tuple(d[p] * states[0][p] + x for p in range(poles)),
-            tuple(d[p] * states[1][p] + u for p in range(poles)),
-        )
-
-    states = ((zero,) * poles, (zero,) * poles)
+    def body(step, states):
+        x = fetch(step)
+        return tuple(d[p] * states[p] + x for p in range(poles))
+
     short = length - SEGS
-    states = repeat(short, 4, body, states)
+    states = repeat(short, 4, body, (zero,) * poles)
     for p in range(poles):
-        ends[1, p * SEGS : (p + 1) * SEGS, :] = states[0][p]
-        heads[1, p * SEGS : (p + 1) * SEGS, :] = states[1][p]
+        ends[1, p * SEGS : (p + 1) * SEGS, :] = states[p]
     for t in range(SEGS):
         states = body(short + t, states)
     for p in range(poles):
-        ends[0, p * SEGS : (p + 1) * SEGS, :] = states[0][p]
-        heads[0, p * SEGS : (p + 1) * SEGS, :] = states[1][p]
-
-
-def link_segments(length, poles, inverse, ends, heads, starts, nexts):
+        ends[0, p * SEGS : (p + 1) * SEGS, :] = states[p]
+
+
+def link_segments(length, poles, order, inverse, ends, starts):
     over = jnp.exp(-float(length) * inverse)
     partial = jnp.exp(-float(length - SEGS) * inverse)
     carried = jnp.zeros_like(inverse)
-    for s in range(SEGS):
+    for s in order:
         starts[s] = carried
-        if s < SEGS - 1:
+        if s != order[-1]:
             carried = over * carried + ends[0, pl.ds(s, poles, stride=SEGS), :]
-    total = partial * carried + ends[1, pl.ds(SEGS - 1, poles, stride=SEGS), :]
-    carried = jnp.zeros_like(inverse)
-    for s in reversed(range(SEGS)):
-        nexts[s] = carried
-        if s:
-            carried = over * carried + heads[0, pl.ds(s, poles, stride=SEGS), :]
-    return total, partial * carried + heads[1, pl.ds(0, poles, stride=SEGS), :]
-
-
-def enter(length, poles, inverse, incoming, after, starts, nexts, begin, finish):
-    for s in range(SEGS):
+    return partial * carried + ends[1, pl.ds(order[-1], poles, stride=SEGS), :]
+
+
+def enter(length, poles, order, inverse, incoming, starts, begin):
+    for rank, s in enumerate(order):
         begin[pl.ds(s, poles, stride=SEGS), :] = (
-            starts[s] + jnp.exp(-float(s * length) * inverse) * incoming
-        )
-        finish[pl.ds(s, poles, stride=SEGS), :] = (
-            nexts[s] + jnp.exp(-float((SEGS - 1 - s) * length) * inverse) * after
+            starts[s] + jnp.exp(-float(rank * length) * inverse) * incoming
         )
 
 
@@ -150,21 +132,10 @@
     repeat(length, 3, body, 0)
 
 
-def stage(rows, taps, before, tok, after, cot, cot_after, natural, cnat, xt, ct):
-    length = rows // SEGS + 1
-    natural[0:HALO, :] = before.astype(jnp.float32)
-    natural[HALO : HALO + rows, :] = tok.astype(jnp.float32)
-    natural[HALO + rows : HALO + rows + HALO, :] = after.astype(jnp.float32)
-    cnat[0:rows, :] = cot.astype(jnp.float32)
-    cnat[rows : rows + HALO, :] = cot_after.astype(jnp.float32)
-    relayout(natural, xt, HALO - (taps - 1), length + taps - 1, length)
-    relayout(cnat, ct, 0, length, length)
-
-
 def kernel(ctxs, grps, poles, taps, tokens, cotangent, w_ref, inv_ref, gain_ref, skip_ref, out,
            tok_in, cot_in, before, after, cot_after, every,
-           natural, cnat, xt, ct, k_at, v_at, src, ups, dq,
-           decay, weights, gain, ends, heads, starts, nexts, begin, finish,
+           natural, cnat, xt, q_at, k_at, v_at, src, ups, dq,
+           decay, weights, gain, ends, starts, nexts, begin,
            send_sem, recv_sem, edge_send, edge_recv, state_send, state_recv):
     ctx, grp = lax.axis_index("ctx"), lax.axis_index("grp")
     share, chans = tokens.shape[0], out.shape[1]
@@ -270,93 +241,129 @@
         edge_copy(1, 0).wait_recv()
         edge_copy(2, 0).wait_recv()
 
-    def state_copy(c, sender, receiver):
+    def state_copy(kind, c, sender, receiver):
         return pltpu.make_async_remote_copy(
-            src_ref=every.at[c, sender],
-            dst_ref=every.at[c, sender],
-            send_sem=state_send.at[c, receiver],
-            recv_sem=state_recv.at[c, sender],
+            src_ref=every.at[kind, c, sender],
+            dst_ref=every.at[kind, c, sender],
+            send_sem=state_send.at[kind, c, receiver],
+            recv_sem=state_recv.at[kind, c, sender],
             device_id=(receiver, grp),
             device_id_type=MESH,
         )
 
+    ahead, behind = tuple(range(SEGS)), tuple(reversed(range(SEGS)))
+
     def here(c):
         return pl.ds(pl.multiple_of(c * LANES, LANES), LANES)
 
-    def phase_one(c):
-        slot = lax.rem(c, 2)
-        for a in range(2):
-            own_copy(a, c).wait()
-            for off in range(1, grps):
-                sender = lax.rem(grp + off, grps)
-                block_copy(a, c, sender, sender).wait_recv()
-        at = here(c)
-        stage(rows, taps, before[:, at], tok_in[c], after[:, at], cot_in[c], cot_after[:, at],
-              natural, cnat, xt, ct.at[slot])
+    def arrive(a, c):
+        own_copy(a, c).wait()
+        for off in range(1, grps):
+            sender = lax.rem(grp + off, grps)
+            block_copy(a, c, sender, sender).wait_recv()
+
+    def tell(kind, c, total):
+        every[kind, c, ctx] = total
+        for off in range(1, ctxs):
+            state_copy(kind, c, ctx, lax.rem(ctx + off, ctxs)).start()
+
+    def hear(kind, c, inverse):
+        for off in range(1, ctxs):
+            sender = lax.rem(ctx + off, ctxs)
+            state_copy(kind, c, sender, sender).wait_recv()
+        over = jnp.exp(-float(rows) * inverse)
+        incoming = jnp.zeros_like(inverse)
+        for j in range(ctxs):
+            if kind == 0:
+                incoming = jnp.where(j < ctx, over * incoming + every[0, c, j], incoming)
+            else:
+                r = ctxs - 1 - j
+                incoming = jnp.where(r > ctx, over * incoming + every[1, c, r], incoming)
+        return incoming
+
+    def token_phase(c):
+        slot, at = lax.rem(c, 2), here(c)
+        arrive(0, c)
+        natural[0:HALO, :] = before[:, at].astype(jnp.float32)
+        natural[HALO : HALO + rows, :] = tok_in[c].astype(jnp.float32)
+        natural[HALO + rows : HALO + rows + HALO, :] = after[:, at].astype(jnp.float32)
+        relayout(natural, xt, HALO - (taps - 1), length + taps - 1, length)
         weights[...] = w_ref[:, :, at]
-        convolve(length, taps, weights, xt, ct.at[slot], None, k_at.at[slot], v_at.at[slot],
-                 src.at[slot], ups.at[slot])
+        convolve(length, taps, weights, xt, q_at, k_at.at[slot], v_at.at[slot], src)
         inverse = inv_ref[:, at]
         decay[...] = jnp.exp(-inverse)
-        local_states(length, poles, decay, src.at[slot], ups.at[slot], ends, heads)
-        total, head = link_segments(
-            length, poles, inverse, ends, heads, starts.at[slot], nexts.at[slot]
-        )
-        every[c, ctx, 0] = total
-        every[c, ctx, 1] = head
-        for off in range(1, ctxs):
-            state_copy(c, ctx, lax.rem(ctx + off, ctxs)).start()
-
-    def phase_two(c):
-        slot = lax.rem(c, 2)
-        for off in range(1, ctxs):
-            sender = lax.rem(ctx + off, ctxs)
-            state_copy(c, sender, sender).wait_recv()
+        local_states(length, poles, decay, lambda t: src[t], ends)
+        tell(0, c, link_segments(length, poles, ahead, inverse, ends, starts))
+
+    def forward_phase(c):
         at = here(c)
+        inverse = inv_ref[:, at]
+        decay[...] = jnp.exp(-inverse)
+        gain[...] = gain_ref[:, at]
+        enter(length, poles, ahead, inverse, hear(0, c, inverse), starts, begin)
+
+        def store(t, value):
+            dq[t] = value
+
+        mix(length, poles, False, decay, gain, skip_ref[:, at], begin, src, store)
+
+    def cotangent_phase(c):
+        at = here(c)
+        arrive(1, c)
+        cnat[0:rows, :] = cot_in[c].astype(jnp.float32)
+        cnat[rows : rows + HALO, :] = cot_after[:, at].astype(jnp.float32)
+        inverse = inv_ref[:, at]
+        decay[...] = jnp.exp(-inverse)
+
+        def fetch(step):
+            t = length - 1 - step
+            value = cnat[pl.ds(t, SEGS, stride=length), :]
+            upstream = value * q_at[t]
+            ups[t] = upstream
+            dq[t] = dq[t] * value
+            return upstream
+
+        local_states(length, poles, decay, fetch, ends)
+        tell(1, c, link_segments(length, poles, behind, inverse, ends, nexts))
+
+    def gradient_phase(c):
+        slot, at = lax.rem(c, 2), here(c)
         weights[...] = w_ref[:, :, at]
         inverse = inv_ref[:, at]
         decay[...] = jnp.exp(-inverse)
         gain[...] = gain_ref[:, at]
-        skip = skip_ref[:, at]
-        over = jnp.exp(-float(rows) * inverse)
-        incoming = jnp.zeros_like(inverse)
-        later = jnp.zeros_like(inverse)
-        for j in range(ctxs):
-            incoming = jnp.where(j < ctx, over * incoming + every[c, j, 0], incoming)
-            r = ctxs - 1 - j
-            later = jnp.where(r > ctx, over * later + every[c, r, 1], later)
-        enter(length, poles, inverse, incoming, later, starts.at[slot], nexts.at[slot], begin, finish)
-        k_here, v_here, c_here = k_at.at[slot], v_at.at[slot], ct.at[slot]
-
-        def store_q(t, value):
-            dq[t] = c_here[t] * value
-
-        def store_kv(t, value):
+        enter(length, poles, behind, inverse, hear(1, c, inverse), nexts, begin)
+        k_here, v_here = k_at.at[slot], v_at.at[slot]
+
+        def store(t, value):
             k, v = k_here[t], v_here[t]
             k_here[t] = value * v
             v_here[t] = value * k
 
-        mix(length, poles, False, decay, gain, skip, begin, src.at[slot], store_q)
-        mix(length, poles, True, decay, gain, skip, finish, ups.at[slot], store_kv)
+        mix(length, poles, True, decay, gain, skip_ref[:, at], begin, ups, store)
         gather_taps(length, taps, weights, (dq, k_here, v_here), natural)
         out[:, at] = natural[0:rows, :].astype(jnp.bfloat16)
 
-    phase_one(0)
-
-    def stagger(c, _):
-        phase_one(c)
-        phase_two(c - 1)
-        return 0
-
-    lax.fori_loop(1, chunks, stagger, 0)
-    phase_two(chunks - 1)
+    def turn(c, _):
+        token_phase(c)
+
+        @pl.when(c > 0)
+        def _():
+            gradient_phase(c - 1)
+
+        forward_phase(c)
+        cotangent_phase(c)
+        return 0
+
+    lax.fori_loop(0, chunks, turn, 0)
+    gradient_phase(jnp.int32(chunks - 1))
 
     def drain(c, _):
         for a in range(2):
             for off in range(1, grps):
                 block_copy(a, c, grp, lax.rem(grp + off, grps)).wait_send()
-        for off in range(1, ctxs):
-            state_copy(c, ctx, lax.rem(ctx + off, ctxs)).wait_send()
+            for off in range(1, ctxs):
+                state_copy(a, c, ctx, lax.rem(ctx + off, ctxs)).wait_send()
         return 0
 
     lax.fori_loop(0, chunks, drain, 0)
@@ -392,7 +399,7 @@
     far = pl.BlockSpec(memory_space=pl.ANY)
     small = pltpu.VMEM((poles * SEGS, LANES), f32)
     pair = pltpu.VMEM((2, poles * SEGS, LANES), f32)
-    linked = pltpu.VMEM((2, SEGS, poles, LANES), f32)
+    linked = pltpu.VMEM((SEGS, poles, LANES), f32)
     edge = pltpu.VMEM((HALO, chans), bf16)
     arrived = pltpu.VMEM((chunks, rows, LANES), bf16)
     natural = pltpu.VMEM((rows + 2 * HALO, LANES), f32)
@@ -403,13 +410,13 @@
         in_specs=[far, far, vmem, vmem, vmem, vmem],
         out_specs=vmem,
         scratch_shapes=[
-            arrived, arrived, edge, edge, edge, pltpu.VMEM((chunks, ctxs, 2, poles, LANES), f32),
-            natural, natural, turned(extra=more), turned(2),
-            turned(2, extra=more), turned(2, extra=more), turned(2), turned(2), turned(extra=more),
+            arrived, arrived, edge, edge, edge, pltpu.VMEM((2, chunks, ctxs, poles, LANES), f32),
+            natural, natural, turned(extra=more), turned(),
+            turned(2, extra=more), turned(2, extra=more), turned(), turned(), turned(extra=more),
             pltpu.VMEM((poles, LANES), f32), pltpu.VMEM((3, taps, LANES), f32),
-            pltpu.VMEM((poles, LANES), f32), pair, pair, linked, linked, small, small,
+            pltpu.VMEM((poles, LANES), f32), pair, linked, linked, small,
             dma((2, chunks, grps)), dma((2, chunks, grps)), dma((3, grps)), dma((3,)),
-            dma((chunks, ctxs)), dma((chunks, ctxs)),
+            dma((2, chunks, ctxs)), dma((2, chunks, ctxs)),
         ],
         compiler_params=pltpu.CompilerParams(
             vmem_limit_bytes=56 * 2**20, collective_id=0, has_side_effects=True

time: 72.7 us -> 72.7 us (level)
  no operation moved by 1% of the time
where the time goes in v4:
time: 72.7 us; the launch traced here: 72.4 us
  Pallas kernels  68.7 us (94%)
  local copies, waits for them, and re-layouts  2.26 us (3%)
  other arithmetic  1.42 us (2%)
    pallas_call x1, Pallas kernels, per_device(): pl.pallas_call(functools.partial(kernel, ctxs, grps, poles, taps), out_sh...  68.7 us
    unnamed x1, local copies, waits for them, and re-layouts  2.26 us

profile of v4, /device:TPU:27, one launch (start us, length us, event | category | flops | bytes accessed | tf_op | source)
XLA Modules:
  0.0 72.4 jit_solution(18281237120060615711)
XLA Ops:
  0.0 1.4 %sqrt_multiply_fusion = (f32[16,512]{1,0:T(8,128)}, f32[16,512]{1,0:T(8,128)}) fusion(f32[16,512]{1,0:T(8,128)} %param.9, f32[16,512]{1,0:T(8,128)} %param.10), kind=kLoop, calls=%fused_computation | loop fusion | flops 32768 | bytes 131072 | tf_op jit(solution)/shard_map/mul | solution.py:391
  1.4 68.7 %shard_map.64 = bf16[1024,512]{1,0:T(8,128)(2,1)} custom-call(bf16[128,4096]{1,0:T(8,128)(2,1)} %tokens.1, bf16[128,4096]{1,0:T(8,128)(2,1)} %cotangent.1, f32[3,7,512]{2,1,0:T(8,128)} %w_ref.1, f32[16,512]{1,0:T(8,128)} %get-tuple-element.6.inv_ref, f32[16,512]{1,0:T(8,128)} %get-tuple-element.5.gain_ref, f32[1,512]{1,0:T(1,128)} %bitcast.1), custom_call_target="tpu_custom_call" | custom-call | tf_op jit(solution)/shard_map/pallas_call | solution.py:407
  70.1 2.3 %copy.8 = bf16[1024,512]{1,0:T(8,128)(2,1)} copy(bf16[1024,512]{1,0:T(8,128)(2,1)} %shard_map.64) | data formatting | bytes 2097152

commit v5 on v4

--- a/solution.py
+++ b/solution.py
@@ -214,14 +214,18 @@
             device_id_type=MESH,
         )
 
-    def send_chunk(c, _):
-        for a in range(2):
-            own_copy(a, c).start()
-            for off in range(1, grps):
-                block_copy(a, c, grp, lax.rem(grp + off, grps)).start()
-        return 0
-
-    lax.fori_loop(0, chunks, send_chunk, 0)
+    def send_blocks(a, c):
+        own_copy(a, c).start()
+        for off in range(1, grps):
+            block_copy(a, c, grp, lax.rem(grp + off, grps)).start()
+
+    def send_next(a, c):
+        @pl.when(c + 1 < chunks)
+        def _():
+            send_blocks(a, c + 1)
+
+    send_blocks(0, 0)
+    send_blocks(1, 0)
 
     @pl.when(first)
     def _():
@@ -284,6 +288,7 @@
     def token_phase(c):
         slot, at = lax.rem(c, 2), here(c)
         arrive(0, c)
+        send_next(0, c)
         natural[0:HALO, :] = before[:, at].astype(jnp.float32)
         natural[HALO : HALO + rows, :] = tok_in[c].astype(jnp.float32)
         natural[HALO + rows : HALO + rows + HALO, :] = after[:, at].astype(jnp.float32)
@@ -310,6 +315,7 @@
     def cotangent_phase(c):
         at = here(c)
         arrive(1, c)
+        send_next(1, c)
         cnat[0:rows, :] = cot_in[c].astype(jnp.float32)
         cnat[rows : rows + HALO, :] = cot_after[:, at].astype(jnp.float32)
         inverse = inv_ref[:, at]

time: 72.7 us -> 71 us (0.977)
  Pallas kernels: 68.7 us -> 67 us
    pallas_call x1, Pallas kernels: 68.7 us -> 67 us  [per_device(): pl.pallas_call(functools.partial(kernel, ctxs, grps, poles, taps), out_sh...]
where the time goes in v5:
time: 71 us; the launch traced here: 70.7 us
  Pallas kernels  67 us (94%)
  local copies, waits for them, and re-layouts  2.26 us (3%)
  other arithmetic  1.42 us (2%)
    pallas_call x1, Pallas kernels, per_device(): pl.pallas_call(functools.partial(kernel, ctxs, grps, poles, taps), out_sh...  67 us
    unnamed x1, local copies, waits for them, and re-layouts  2.26 us
    mul x1, other arithmetic, per_device(): gain = residue * jnp.sqrt(-jnp.expm1(-2.0 * inverse))  1.42 us

profile of v5, /device:TPU:27, one launch (start us, length us, event | category | flops | bytes accessed | tf_op | source)
XLA Modules:
  0.0 70.7 jit_solution(16084873171130631633)
XLA Ops:
  0.0 1.4 %sqrt_multiply_fusion = (f32[16,512]{1,0:T(8,128)}, f32[16,512]{1,0:T(8,128)}) fusion(f32[16,512]{1,0:T(8,128)} %param.9, f32[16,512]{1,0:T(8,128)} %param.10), kind=kLoop, calls=%fused_computation | loop fusion | flops 32768 | bytes 131072 | tf_op jit(solution)/shard_map/mul | solution.py:397
  1.4 67.0 %shard_map.64 = bf16[1024,512]{1,0:T(8,128)(2,1)} custom-call(bf16[128,4096]{1,0:T(8,128)(2,1)} %tokens.1, bf16[128,4096]{1,0:T(8,128)(2,1)} %cotangent.1, f32[3,7,512]{2,1,0:T(8,128)} %w_ref.1, f32[16,512]{1,0:T(8,128)} %get-tuple-element.6.inv_ref, f32[16,512]{1,0:T(8,128)} %get-tuple-element.5.gain_ref, f32[1,512]{1,0:T(1,128)} %bitcast.1), custom_call_target="tpu_custom_call" | custom-call | tf_op jit(solution)/shard_map/pallas_call | solution.py:413
  68.4 2.3 %copy.8 = bf16[1024,512]{1,0:T(8,128)(2,1)} copy(bf16[1024,512]{1,0:T(8,128)(2,1)} %shard_map.64) | data formatting | bytes 2097152

commit v6 on v5

--- a/solution.py
+++ b/solution.py
@@ -73,7 +73,7 @@
         return tuple(d[p] * states[p] + x for p in range(poles))
 
     short = length - SEGS
-    states = repeat(short, 4, body, (zero,) * poles)
+    states = repeat(short, 8, body, (zero,) * poles)
     for p in range(poles):
         ends[1, p * SEGS : (p + 1) * SEGS, :] = states[p]
     for t in range(SEGS):
@@ -113,7 +113,7 @@
         store(t, tree_sum([g[p] * states[p] for p in range(poles)] + [skip * x]))
         return states
 
-    repeat(length, 4, body, states)
+    repeat(length, 8, body, states)
 
 
 def gather_taps(length, taps, w_ref, streams, natural):

time: 71 us -> 70.6 us (level)
  no operation moved by 1% of the time
where the time goes in v6:
time: 70.6 us; the launch traced here: 70.3 us
  Pallas kernels  66.6 us (94%)
  local copies, waits for them, and re-layouts  2.26 us (3%)
  other arithmetic  1.42 us (2%)
    pallas_call x1, Pallas kernels, per_device(): pl.pallas_call(functools.partial(kernel, ctxs, grps, poles, taps), out_sh...  66.6 us
    unnamed x1, local copies, waits for them, and re-layouts  2.26 us
    mul x1, other arithmetic, per_device(): gain = residue * jnp.sqrt(-jnp.expm1(-2.0 * inverse))  1.42 us

profile of v6, /device:TPU:27, one launch (start us, length us, event | category | flops | bytes accessed | tf_op | source)
XLA Modules:
  0.0 70.3 jit_solution(1759188178193539461)
XLA Ops:
  0.0 1.4 %sqrt_multiply_fusion = (f32[16,512]{1,0:T(8,128)}, f32[16,512]{1,0:T(8,128)}) fusion(f32[16,512]{1,0:T(8,128)} %param.9, f32[16,512]{1,0:T(8,128)} %param.10), kind=kLoop, calls=%fused_computation | loop fusion | flops 32768 | bytes 131072 | tf_op jit(solution)/shard_map/mul | solution.py:397
  1.4 66.6 %shard_map.64 = bf16[1024,512]{1,0:T(8,128)(2,1)} custom-call(bf16[128,4096]{1,0:T(8,128)(2,1)} %tokens.1, bf16[128,4096]{1,0:T(8,128)(2,1)} %cotangent.1, f32[3,7,512]{2,1,0:T(8,128)} %w_ref.1, f32[16,512]{1,0:T(8,128)} %get-tuple-element.6.inv_ref, f32[16,512]{1,0:T(8,128)} %get-tuple-element.5.gain_ref, f32[1,512]{1,0:T(1,128)} %bitcast.1), custom_call_target="tpu_custom_call" | custom-call | tf_op jit(solution)/shard_map/pallas_call | solution.py:413
  68.0 2.3 %copy.8 = bf16[1024,512]{1,0:T(8,128)(2,1)} copy(bf16[1024,512]{1,0:T(8,128)(2,1)} %shard_map.64) | data formatting | bytes 2097152
